TPU v7x, 32 devices: a whole 2x2x4 slice. The times are simulated.
32 devices in a mesh: dp: 8 (over y, x, core), tensor: 4 (over z).
Axes of the slice: x: 2, y: 2, z: 4, core: 2. Of those that a mesh axis runs over, the one named last changes fastest.
Arguments:
- hidden_in: bfloat16 [16, 1024, 1024], P('dp', 'tensor'), may hold values from -6 to 6
- segments: int32 [16, 1024], P('dp'), may hold values from 0 to 2, as said below
- ln1_gain: bfloat16 [1024], replicated, may hold values from 0.5 to 1.5
- ln1_bias: bfloat16 [1024], replicated, may hold values from -3 to 3
- ln2_gain: bfloat16 [1024], replicated, may hold values from 0.5 to 1.5
- ln2_bias: bfloat16 [1024], replicated, may hold values from -3 to 3
- w_qkv: bfloat16 [3, 1024, 1024], P(None, 'dp', 'tensor'), may hold values from -0.1875 to 0.1875
- b_qkv: bfloat16 [3, 1024], replicated, may hold values from -6 to 6
- w_out: bfloat16 [1024, 1024], P('dp', 'tensor'), may hold values from -0.75 to 0.75
- b_out: bfloat16 [1024], replicated, may hold values from -4 to 4
- w_up: bfloat16 [1024, 4096], P('dp', 'tensor'), may hold values from -0.1875 to 0.1875
- b_up: bfloat16 [4096], replicated, may hold values from -6 to 6
- w_down: bfloat16 [1024, 4096], P('dp', 'tensor'), may hold values from -0.09375 to 0.09375
- b_down: bfloat16 [1024], replicated, may hold values from -4 to 4
- cotangent: bfloat16 [16, 1024, 1024], P('dp', 'tensor'), may hold values from -6 to 6
Outputs:
- block_out: bfloat16 [16, 1024, 1024], P('dp', 'tensor')
- grad_in: bfloat16 [16, 1024, 1024], P('dp', 'tensor')
- grad_ln1_gain: float32 [1024], replicated
- grad_ln1_bias: float32 [1024], replicated
- grad_ln2_gain: float32 [1024], replicated
- grad_ln2_bias: float32 [1024], replicated
- grad_w_qkv: float32 [3, 1024, 1024], P(None, 'dp', 'tensor')
- grad_b_qkv: float32 [3, 1024], replicated
- grad_w_out: float32 [1024, 1024], P('dp', 'tensor')
- grad_b_out: float32 [1024], replicated
- grad_w_up: float32 [1024, 4096], P('dp', 'tensor')
- grad_b_up: float32 [4096], replicated
- grad_w_down: float32 [1024, 4096], P('dp', 'tensor')
- grad_b_down: float32 [1024], replicated
Inputs may be any that keep to these rules, and one draw needn't show every extreme that they name: `segments`: segment numbers start at 0 in every sequence and never fall along it; of the 2 sequences of each index of dp, one holds a single document.
All inputs are finite; a program needn't handle non-finite values.
Results may differ from a plain program's by a relative error of at most 0.0097.
Values may be sent and summed in bfloat16 or wider, within the bound.
A program may use at most 128 MiB of HBM per device.

v0:
```python
import math

import jax
import jax.numpy as jnp
from jax import lax
from jax.sharding import PartitionSpec as P

HEAD_DIM = 64
ROT = 16


EPSILON = 1e-05


def doc_positions(segment_ids):
    length_all = segment_ids.shape[-1]
    places = jnp.broadcast_to(jnp.arange(length_all, dtype=jnp.int32), segment_ids.shape)
    first_flag = jnp.ones(segment_ids.shape[:-1] + (1,), jnp.bool_)
    starts = jnp.concatenate([first_flag, segment_ids[..., 1:] != segment_ids[..., :-1]], -1)
    begins = lax.cummax(jnp.where(starts, places, 0), axis=segment_ids.ndim - 1)
    return places - begins


def rotary_tables(positions):
    frequency = 10000.0 ** (-jnp.arange(ROT // 2, dtype=jnp.float32) * (2.0 / ROT))
    angles = positions.astype(jnp.float32)[..., None] * frequency
    return (jnp.cos(angles)[..., None, :], jnp.sin(angles)[..., None, :])


def rotate(vectors, cosine_table, sine_table, direction):
    first_half = vectors[..., : ROT // 2]
    second_half = vectors[..., ROT // 2 : ROT]
    untouched = vectors[..., ROT:]
    return jnp.concatenate(
        [
            first_half * cosine_table - direction * second_half * sine_table,
            second_half * cosine_table + direction * first_half * sine_table,
            untouched,
        ],
        -1,
    )


def gelu_slope(inputs_now):
    cumulative = 0.5 * (1.0 + jax.scipy.special.erf(inputs_now * (1.0 / math.sqrt(2.0))))
    density = jnp.exp(-0.5 * inputs_now * inputs_now) * (1.0 / math.sqrt(2.0 * math.pi))
    return cumulative + inputs_now * density


def layer_normed(hidden):
    centred = hidden - jnp.mean(hidden, -1, keepdims=True)
    scaling = lax.rsqrt(jnp.mean(centred * centred, -1, keepdims=True) + EPSILON)
    return (centred * scaling, scaling)


def mask_for(segment_rows, segment_ids, row_start):
    rows_here = row_start + jnp.arange(segment_rows.shape[0], dtype=jnp.int32)
    columns = jnp.arange(segment_ids.shape[0], dtype=jnp.int32)
    return (columns[None, :] <= rows_here[:, None]) & (
        segment_ids[None, :] == segment_rows[:, None]
    )


def attend_forward(query_block, keys_all, values, allowed):
    scores = jnp.einsum("ihd,jhd->hij", query_block, keys_all, preferred_element_type=jnp.float32)
    scores = jnp.where(allowed[None], scores, -1e30)
    largest = jnp.max(scores, -1, keepdims=True)
    powered = jnp.exp(scores - largest)
    totals = jnp.sum(powered, -1, keepdims=True)
    weights = (powered / totals).astype(jnp.bfloat16)
    output = jnp.einsum("hij,jhd->ihd", weights, values, preferred_element_type=jnp.float32)
    return (output.astype(jnp.bfloat16), (largest + jnp.log(totals))[..., 0])


def attend_backward(query_block, keys_all, values, grad_block, log_block, allowed):
    scores = jnp.einsum("ihd,jhd->hij", query_block, keys_all, preferred_element_type=jnp.float32)
    probabilities = jnp.where(allowed[None], jnp.exp(scores - log_block[..., None]), 0.0)
    grad_probs = jnp.einsum("ihd,jhd->hij", grad_block, values, preferred_element_type=jnp.float32)
    inner_sum = jnp.sum(probabilities * grad_probs, -1, keepdims=True)
    grad_scores = (probabilities * (grad_probs - inner_sum)).astype(jnp.bfloat16)
    grad_query = jnp.einsum(
        "hij,jhd->ihd", grad_scores, keys_all, preferred_element_type=jnp.float32
    )
    grad_keys = jnp.einsum(
        "hij,ihd->jhd", grad_scores, query_block, preferred_element_type=jnp.float32
    )
    grad_values = jnp.einsum(
        "hij,ihd->jhd",
        probabilities.astype(jnp.bfloat16),
        grad_block,
        preferred_element_type=jnp.float32,
    )
    return (grad_query, grad_keys, grad_values)


def forward_sequence(members):
    queries, keys_all, values, segment_ids = members
    block_rows = min(512, queries.shape[0])
    starts = jnp.arange(queries.shape[0] // block_rows, dtype=jnp.int32) * block_rows

    def one_block(row_start):
        query_block = lax.dynamic_slice_in_dim(queries, row_start, block_rows, 0)
        segment_rows = lax.dynamic_slice_in_dim(segment_ids, row_start, block_rows, 0)
        return attend_forward(
            query_block, keys_all, values, mask_for(segment_rows, segment_ids, row_start)
        )

    outputs, log_totals = lax.map(one_block, starts)
    return (outputs.reshape(queries.shape), log_totals)


def backward_sequence(members):
    queries, keys_all, values, grad_out, log_totals, segment_ids = members
    block_rows = min(512, queries.shape[0])
    starts = jnp.arange(queries.shape[0] // block_rows, dtype=jnp.int32) * block_rows

    def advance(running, inputs_now):
        row_start, log_block = inputs_now
        query_block = lax.dynamic_slice_in_dim(queries, row_start, block_rows, 0)
        grad_block = lax.dynamic_slice_in_dim(grad_out, row_start, block_rows, 0)
        segment_rows = lax.dynamic_slice_in_dim(segment_ids, row_start, block_rows, 0)
        allowed = mask_for(segment_rows, segment_ids, row_start)
        grad_query, grad_keys, grad_values = attend_backward(
            query_block, keys_all, values, grad_block, log_block, allowed
        )
        return ((running[0] + grad_keys, running[1] + grad_values), grad_query)

    zero_keys = jnp.zeros(keys_all.shape, jnp.float32)
    (grad_keys, grad_values), grad_queries = lax.scan(
        advance, (zero_keys, zero_keys), (starts, log_totals)
    )
    return (grad_queries.reshape(keys_all.shape), grad_keys, grad_values)


def shards(
    hidden_in,
    segments,
    ln1_gain,
    ln1_bias,
    ln2_gain,
    ln2_bias,
    w_qkv,
    b_qkv,
    w_out,
    b_out,
    w_up,
    b_up,
    w_down,
    b_down,
    cotangent,
):
    seq_count = hidden_in.shape[0]
    length_all = segments.shape[1]
    model_width = hidden_in.shape[2]
    row_total = seq_count * length_all
    tensor_index = lax.axis_index("tensor")
    scale_query = 1.0 / math.sqrt(HEAD_DIM)
    by_columns = (((1,), (1,)), ((), ()))
    by_rows = (((0,), (0,)), ((), ()))
    hidden = hidden_in.astype(jnp.float32)
    normed, scaling = layer_normed(hidden)
    first_in = (normed * ln1_gain + ln1_bias).astype(jnp.bfloat16)
    second_in = (normed * ln2_gain + ln2_bias).astype(jnp.bfloat16)
    first_all, second_all = (
        lax.all_gather(first_in, "tensor", axis=1, tiled=True),
        lax.all_gather(second_in, "tensor", axis=1, tiled=True),
    )
    full_qkv, full_out, full_up, full_down = (
        lax.all_gather(w_qkv, "dp", axis=1, tiled=True),
        lax.all_gather(w_out, "dp", axis=0, tiled=True),
        lax.all_gather(w_up, "dp", axis=0, tiled=True),
        lax.all_gather(w_down, "dp", axis=0, tiled=True),
    )
    local_width = full_qkv.shape[2]
    local_heads = local_width // HEAD_DIM
    local_units = full_up.shape[1]
    first_rows = first_all.reshape(row_total, model_width)
    second_rows = second_all.reshape(row_total, model_width)
    bias_qkv = lax.dynamic_slice_in_dim(b_qkv, tensor_index * local_width, local_width, 1)
    bias_up = lax.dynamic_slice_in_dim(b_up, tensor_index * local_units, local_units, 0)
    projected = (
        jnp.einsum("rd,cde->cre", first_rows, full_qkv, preferred_element_type=jnp.float32)
        + bias_qkv[:, None, :]
    )
    cosine_table, sine_table = rotary_tables(doc_positions(segments).reshape(row_total))
    row_heads = (row_total, local_heads, HEAD_DIM)
    head_shape = (seq_count, length_all, local_heads, HEAD_DIM)
    queries = (
        (rotate(projected[0].reshape(row_heads), cosine_table, sine_table, 1.0) * scale_query)
        .astype(jnp.bfloat16)
        .reshape(head_shape)
    )
    keys_all = (
        rotate(projected[1].reshape(row_heads), cosine_table, sine_table, 1.0)
        .astype(jnp.bfloat16)
        .reshape(head_shape)
    )
    values = projected[2].astype(jnp.bfloat16).reshape(head_shape)
    attended, log_totals = lax.map(forward_sequence, (queries, keys_all, values, segments))
    attended_rows = attended.reshape(row_total, local_width)
    units = jnp.dot(second_rows, full_up, preferred_element_type=jnp.float32) + bias_up
    activated = jax.nn.gelu(units, approximate=False).astype(jnp.bfloat16)
    branch_terms = lax.dot_general(
        attended_rows, full_out, by_columns, preferred_element_type=jnp.float32
    )
    branch_terms = branch_terms + lax.dot_general(
        activated, full_down, by_columns, preferred_element_type=jnp.float32
    )
    branch_sum = lax.psum_scatter(
        branch_terms.reshape(seq_count, length_all, model_width),
        "tensor",
        scatter_dimension=1,
        tiled=True,
    )
    block_out = (hidden + branch_sum + b_out + b_down).astype(jnp.bfloat16)
    cot_all = lax.all_gather(cotangent, "tensor", axis=1, tiled=True)
    cot_rows = cot_all.reshape(row_total, model_width)
    back_qkv, back_out, back_up, back_down = (
        lax.all_gather(w_qkv, "dp", axis=1, tiled=True),
        lax.all_gather(w_out, "dp", axis=0, tiled=True),
        lax.all_gather(w_up, "dp", axis=0, tiled=True),
        lax.all_gather(w_down, "dp", axis=0, tiled=True),
    )
    grad_attended = jnp.dot(cot_rows, back_out, preferred_element_type=jnp.float32).astype(
        jnp.bfloat16
    )
    grad_units = (
        jnp.dot(cot_rows, back_down, preferred_element_type=jnp.float32) * gelu_slope(units)
    ).astype(jnp.bfloat16)
    grad_query_raw, grad_keys_raw, grad_values_raw = lax.map(
        backward_sequence,
        (queries, keys_all, values, grad_attended.reshape(head_shape), log_totals, segments),
    )
    grad_queries = rotate(
        grad_query_raw.reshape(row_heads) * scale_query, cosine_table, sine_table, -1.0
    )
    grad_keys = rotate(grad_keys_raw.reshape(row_heads), cosine_table, sine_table, -1.0)
    grad_projected = jnp.stack(
        [
            grad_queries.reshape(row_total, local_width),
            grad_keys.reshape(row_total, local_width),
            grad_values_raw.reshape(row_total, local_width),
        ]
    ).astype(jnp.bfloat16)
    part_qkv = jnp.einsum(
        "rd,cre->cde", first_rows, grad_projected, preferred_element_type=jnp.float32
    )
    part_out = lax.dot_general(cot_rows, attended_rows, by_rows, preferred_element_type=jnp.float32)
    part_up = lax.dot_general(second_rows, grad_units, by_rows, preferred_element_type=jnp.float32)
    part_down = lax.dot_general(cot_rows, activated, by_rows, preferred_element_type=jnp.float32)
    grad_w_qkv, grad_w_out, grad_w_up, grad_w_down = (
        lax.psum_scatter(part_qkv, "dp", scatter_dimension=1, tiled=True),
        lax.psum_scatter(part_out, "dp", scatter_dimension=0, tiled=True),
        lax.psum_scatter(part_up, "dp", scatter_dimension=0, tiled=True),
        lax.psum_scatter(part_down, "dp", scatter_dimension=0, tiled=True),
    )
    grad_first = jnp.einsum(
        "cre,cde->rd", grad_projected, back_qkv, preferred_element_type=jnp.float32
    )
    grad_second = lax.dot_general(
        grad_units, back_up, by_columns, preferred_element_type=jnp.float32
    )
    grad_first_own, grad_second_own = (
        lax.psum_scatter(
            grad_first.reshape(seq_count, length_all, model_width),
            "tensor",
            scatter_dimension=1,
            tiled=True,
        ),
        lax.psum_scatter(
            grad_second.reshape(seq_count, length_all, model_width),
            "tensor",
            scatter_dimension=1,
            tiled=True,
        ),
    )
    norm_terms = (
        jnp.sum(grad_first_own * normed, (0, 1)),
        jnp.sum(grad_first_own, (0, 1)),
        jnp.sum(grad_second_own * normed, (0, 1)),
        jnp.sum(grad_second_own, (0, 1)),
    )
    grad_normed = grad_first_own * ln1_gain + grad_second_own * ln2_gain
    grad_hidden = cotangent.astype(jnp.float32) + scaling * (
        grad_normed
        - jnp.mean(grad_normed, -1, keepdims=True)
        - normed * jnp.mean(grad_normed * normed, -1, keepdims=True)
    )
    qkv_sums = jnp.sum(grad_projected, 1, dtype=jnp.float32)
    padded_qkv = lax.dynamic_update_slice_in_dim(
        jnp.zeros((3, model_width), jnp.float32), qkv_sums, tensor_index * local_width, 1
    )
    unit_sums = jnp.sum(grad_units, 0, dtype=jnp.float32)
    padded_up = lax.dynamic_update_slice_in_dim(
        jnp.zeros((b_up.shape[0],), jnp.float32), unit_sums, tensor_index * local_units, 0
    )
    cot_sums = jnp.sum(cotangent, (0, 1), dtype=jnp.float32)
    small_sums = lax.psum(
        (
            norm_terms[0],
            norm_terms[1],
            norm_terms[2],
            norm_terms[3],
            padded_qkv,
            cot_sums,
            padded_up,
        ),
        ("dp", "tensor"),
    )
    return (
        block_out,
        grad_hidden.astype(jnp.bfloat16),
        small_sums[0],
        small_sums[1],
        small_sums[2],
        small_sums[3],
        grad_w_qkv,
        small_sums[4],
        grad_w_out,
        small_sums[5],
        grad_w_up,
        small_sums[6],
        grad_w_down,
        small_sums[5],
    )


def solution(mesh):
    in_specs = (
        P("dp", "tensor", None),
        P("dp", None),
        P(),
        P(),
        P(),
        P(),
        P(None, "dp", "tensor"),
        P(),
        P("dp", "tensor"),
        P(),
        P("dp", "tensor"),
        P(),
        P("dp", "tensor"),
        P(),
        P("dp", "tensor", None),
    )
    out_specs = (
        P("dp", "tensor", None),
        P("dp", "tensor", None),
        P(),
        P(),
        P(),
        P(),
        P(None, "dp", "tensor"),
        P(),
        P("dp", "tensor"),
        P(),
        P("dp", "tensor"),
        P(),
        P("dp", "tensor"),
        P(),
    )
    return jax.shard_map(shards, mesh=mesh, in_specs=in_specs, out_specs=out_specs, check_vma=False)
```

profile of v0, /device:TPU:0, one launch (start us, length us, event | category | flops | bytes accessed | tf_op | source)
XLA Modules:
  0.0 1039.5 jit_solution(3583430998072355343)
XLA Ops:
  15.0 3.2 fusion.62
  21.9 12.3 %all_gather.27 = bf16[1024,256]{1,0:T(8,128)(2,1)} all-gather(bf16[128,256]{1,0:T(8,128)(2,1)S(1)} %copy-done.19), channel_id=1, replica_groups=mesh['dp'=8,'tensor'=4] {'dp'}, dimensions={0}, use_global_device_ids=true | all-gather | bytes 589824 | tf_op jit(solution)/shard_map/all_gather | solution.py:170
  39.1 83.2 %all-gather.7.cloned.1.call-done = bf16[2,1024,1024]{2,1,0:T(8,128)(2,1)} async-done(((bf16[2,256,1024]{2,1,0:T(8,128)(2,1)}), bf16[2,1024,1024]{2,1,0:T(8,128)(2,1)}) %all-gather.7.cloned.1.call-update) | async-done | bytes 4194320 | tf_op jit(solution)/shard_map/all_gather | solution.py:165
  122.2 5.7 add_bitcast_fusion
  130.1 3.3 concatenate.39
  137.1 3.1 copy.56
  140.2 3.0 copy.57
  143.2 3.1 copy.83
  146.3 7.4 fusion.52
  158.1 49.6 %while.54 = (s32[]{:T(128)}, bf16[2,1024,4,64]{3,2,1,0:T(4,128)(2,1)}, f32[2,2,4,512]{3,2,1,0:T(4,128)S(1)}, bf16[2,1024,4,64]{1,3,2,0:T(8,128)(2,1)}, s32[2,102...) while((s32[]{:T(128)}, ...), condition=%wide.region_9.10_spmd, body=%wide.region_4.9_spmd.sunk | while | flops 557447680 | bytes 34724764 | solution.py:199
  160.7 20.2 %while.57 = (s32[]{:T(128)}, bf16[2,512,4,64]{1,3,2,0:T(8,128)(2,1)S(1)}, f32[2,4,512]{2,1,0:T(4,128)S(1)}, s32[2]{0:T(128)S(1)}, s32[1024]{0:T(1024)S(1)}, /*in...) while((s32[]{:T(128)}, ...), condition=%wide.region_8.8_spmd, body=%wide.region_5.7_spmd.sunk | while | flops 557447680 | bytes 28915888 | solution.py:108
  185.4 20.2 %while.57 = (s32[]{:T(128)}, bf16[2,512,4,64]{1,3,2,0:T(8,128)(2,1)S(1)}, f32[2,4,512]{2,1,0:T(4,128)S(1)}, s32[2]{0:T(128)S(1)}, s32[1024]{0:T(1024)S(1)}, /*in...) while((s32[]{:T(128)}, ...), condition=%wide.region_8.8_spmd, body=%wide.region_5.7_spmd.sunk | while | flops 557447680 | bytes 28915888 | solution.py:108
  207.7 4.5 convolution_convert_fusion
  212.2 3.3 reshape.329
  217.9 159.4 %while.56 = (s32[]{:T(128)}, f32[2,1024,4,64]{3,2,1,0:T(4,128)}, f32[2,1024,4,64]{1,0,3,2:T(2,128)}, bf16[2,1024,4,64]{1,3,2,0:T(8,128)(2,1)}, f32[2,2,4,512]{3,...) while((s32[]{:T(128)}, f32[2,1024,4,64]{3,2,1,0:T(4,128)}, ...), condition=%wide.region_15.16_spmd, body=%wide.region_11.15_spmd.sunk | while | flops 1369963008 | bytes 171032272 | solution.py:230
  222.5 47.9 %while.58 = (s32[]{:T(128)}, f32[1024,4,64]{0,2,1:T(8,128)S(1)}, f32[1024,4,64]{0,2,1:T(8,128)S(1)}, f32[2,512,4,64]{1,3,2,0:T(8,128)}, s32[2]{0:T(128)S(1)}, /*...) while((s32[]{:T(128)}, f32[1024,4,64]{0,2,1:T(8,128)S(1)}, ...), condition=%wide.region_14.14_spmd.clone, body=%wide.region_12.13_spmd.clone.sunk | while | flops 1369963008 | bytes 154212768 | solution.py:129
  228.8 3.1 multiply_reduce_fusion.2
  232.0 3.5 multiply_convert_fusion.2
  235.4 3.4 fusion.145
  238.9 4.9 fusion.147
  253.0 3.1 multiply_reduce_fusion.2
  256.2 3.5 multiply_convert_fusion.2
  259.7 3.5 fusion.145
  263.1 4.3 fusion.147
  270.4 2.7 copy.115
  273.1 3.1 bitcast_dynamic-update-slice_fusion.12
  278.3 18.8 %dynamic_update_slice.59 = f32[2,1024,4,64]{1,0,3,2:T(2,128)} dynamic-update-slice(f32[2,1024,4,64]{1,0,3,2:T(2,128)} %get-tuple-element.860, f32[1,1024,4,64]{1,0,3,2:T(1,128)} %copy.116, s32[]{:T(128)} %get-tuple-element.858, s32[]{:T(128)} %constant.91.clone.1..sunk.2, s32[]{:T(128)} %constant.91.clone.1..sunk.2, s32[]{:T(128)} %constant.91.clone.1..sunk.2) | dynamic-update-slice | bytes 2097156 | tf_op jit(solution)/shard_map/while/body/jit(dynamic_update_index_in_dim)/dynamic_update_slice | solution.py:230
  302.4 47.4 %while.58 = (s32[]{:T(128)}, f32[1024,4,64]{0,2,1:T(8,128)S(1)}, f32[1024,4,64]{0,2,1:T(8,128)S(1)}, f32[2,512,4,64]{1,3,2,0:T(8,128)}, s32[2]{0:T(128)S(1)}, /*...) while((s32[]{:T(128)}, f32[1024,4,64]{0,2,1:T(8,128)S(1)}, ...), condition=%wide.region_14.14_spmd.clone, body=%wide.region_12.13_spmd.clone.sunk | while | flops 1369963008 | bytes 154212768 | solution.py:129
  308.7 3.1 multiply_reduce_fusion.2
  311.9 3.5 multiply_convert_fusion.2
  315.4 3.4 fusion.145
  318.8 4.3 fusion.147
  332.4 3.1 multiply_reduce_fusion.2
  335.6 3.5 multiply_convert_fusion.2
  339.0 3.5 fusion.145
  342.5 4.2 fusion.147
  349.8 2.7 copy.115
  352.5 3.1 bitcast_dynamic-update-slice_fusion.12
  357.7 18.8 %dynamic_update_slice.59 = f32[2,1024,4,64]{1,0,3,2:T(2,128)} dynamic-update-slice(f32[2,1024,4,64]{1,0,3,2:T(2,128)} %get-tuple-element.860, f32[1,1024,4,64]{1,0,3,2:T(1,128)} %copy.116, s32[]{:T(128)} %get-tuple-element.858, s32[]{:T(128)} %constant.91.clone.1..sunk.2, s32[]{:T(128)} %constant.91.clone.1..sunk.2, s32[]{:T(128)} %constant.91.clone.1..sunk.2) | dynamic-update-slice | bytes 2097156 | tf_op jit(solution)/shard_map/while/body/jit(dynamic_update_index_in_dim)/dynamic_update_slice | solution.py:230
  377.3 3.9 reshape.328
  381.2 4.4 convolution_bitcast_fusion.4
  385.6 5.2 broadcast_multiply_fusion
  390.9 8.0 fusion.82
  400.1 3.5 copy.103
  403.6 4.4 copy.104
  408.0 4.1 reshape.323
  421.1 2.9 copy.88
  426.1 8.3 convolution_bitcast_fusion.3
  434.6 25.4 %fusion.38 = (bf16[2048,1024]{1,0:T(8,128)(2,1)S(1)}, f32[2048,1024]{1,0:T(8,128)}) fusion(f32[1024]{0:T(1024)S(1)} %copy-done.29, bf16[2048,1024]{1,0:T(8,128)(2,1)} %bitcast.209, bf16[1024,1024]{1,0:T(8,128)(2,1)} %all-gather.13.cloned.1.call-done), kind=kOutput, calls=%fused_computation.65 | convolution fusion | flops 4433379328 | bytes 18878464 | tf_op jit(solution)/shard_map/dot_general | solution.py:201
  462.0 6.1 convolution_bitcast_fusion.2
  469.7 8.4 fusion.77
  478.2 11.6 %convert_reduce_fusion = (f32[1024]{0:T(1024)S(1)}, bf16[2048,1024]{1,0:T(8,128)(2,1)S(1)}) fusion(f32[2048,1024]{1,0:T(8,128)} %get-tuple-element.437, f32[1024]{0:T(1024)S(1)} %copy-done.29, bf16[2048,1024]{1,0:T(8,128)(2,1)} %bitcast.213, bf16[1024,1024]{1,0:T(8,128)(2,1)} %all-gather.15.cloned.1.call-done), kind=kOutput, calls=%fused_computation.72 | convolution fusion | flops 4322229248 | bytes 18882560 | tf_op jit(solution)/shard_map/dot_general | solution.py:228
  489.8 6.9 fusion.84
  496.8 7.1 fusion.83
  503.8 4.7 convolution_add_fusion
  508.8 10.2 fusion.85
  525.7 8.3 reduce-scatter.20.cloned.1.call-done
  536.0 144.6 %reduce-scatter.10.cloned.1.call-done = f32[2,256,1024]{2,1,0:T(8,128)} async-done(((f32[2,1024,1024]{2,1,0:T(8,128)}), f32[2,256,1024]{2,1,0:T(8,128)}) %reduce-scatter.10.cloned.1.call-update) | async-done | bytes 2097168 | tf_op jit(solution)/shard_map/reduce_scatter | solution.py:264
  680.7 147.6 %reduce-scatter.12.cloned.1.call-done = f32[2,256,1024]{2,1,0:T(8,128)} async-done(((f32[2,1024,1024]{2,1,0:T(8,128)}), f32[2,256,1024]{2,1,0:T(8,128)}) %reduce-scatter.12.cloned.1.call-update) | async-done | bytes 2097168 | tf_op jit(solution)/shard_map/reduce_scatter | solution.py:270
  828.3 3.0 fusion.78
  831.3 144.4 %reduce-scatter.8.cloned.1.call-done = f32[2,256,1024]{2,1,0:T(8,128)} async-done(((f32[2,1024,1024]{2,1,0:T(8,128)}), f32[2,256,1024]{2,1,0:T(8,128)}) %reduce-scatter.8.cloned.1.call-update) | async-done | bytes 2097168 | tf_op jit(solution)/shard_map/reduce_scatter | solution.py:209
  975.7 3.6 convert_reduce_fusion.3
  979.3 42.3 %all-reduce.1 = (f32[1024]{0:T(1024)}, f32[1024]{0:T(1024)}, f32[1024]{0:T(1024)}, f32[1024]{0:T(1024)}, f32[3,1024]{1,0:T(4,128)}, /*index=5*/f32[1024]{0:T(1024)S(1)}, f32[4096]{0:T(1024)}) all-reduce(f32[1024]{0:T(1024)S(1)} %get-tuple-element.414, ...), channel_id=1, replica_groups=mesh['dp'=8,'tensor'=4] {'dp','tensor'}, use_global_device_ids=true, to_apply=%region_21.22 | all-reduce | flops 12288 | bytes 98304 | tf_op jit(solution)/shard_map/psum | solution.py:298
  1021.6 10.3 reduce-scatter.18.cloned.1.call-done
  (305 shorter events, 139.6 us)
Async XLA Ops:
  7.2 31.9 %all-gather.9.cloned.1.call-start = ((), (), s32[]{:S(2)}) async-start(), calls=%async_computation.8 | async-start | bytes 1769472 | tf_op jit(solution)/shard_map/all_gather | solution.py:169
  9.0 113.2 %all-gather.7.cloned.1.call-start = ((), (), s32[]{:S(2)}) async-start(), calls=%async_computation.7 | async-start | bytes 5242880 | tf_op jit(solution)/shard_map/all_gather | solution.py:165
  9.7 10.3 copy-start.22
  10.4 9.7 copy-start.24
  13.2 7.6 copy-start.16
  13.2 8.7 copy-start.19
  13.3 21.0 %copy-start.20 = (f32[2,256]{1,0:T(2,128)}, f32[2,256]{1,0:T(2,128)S(1)}, u32[]{:S(2)}) copy-start(f32[2,256]{1,0:T(2,128)S(1)} %broadcast_multiply_fusion.4) | copy-start | bytes 6148
  14.9 113.0 %copy-start.26 = (f32[2,256]{1,0:T(2,128)}, f32[2,256]{1,0:T(2,128)S(1)}, u32[]{:S(2)}) copy-start(f32[2,256]{1,0:T(2,128)S(1)} %add_rsqrt_fusion) | copy-start | bytes 6148
  18.2 189.5 %all-gather.17.cloned.1.call-start = ((), (), s32[]{:S(2)}) async-start(), calls=%async_computation.13 | async-start | bytes 5242880 | tf_op jit(solution)/shard_map/all_gather | solution.py:216
  18.9 415.7 %all-gather.13.cloned.1.call-start = ((), (), s32[]{:S(2)}) async-start(), calls=%async_computation.10 | async-start | bytes 2359296 | tf_op jit(solution)/shard_map/all_gather | solution.py:171
  19.5 415.1 %all-gather.11.cloned.1.call-start = ((), (), s32[]{:S(2)}) async-start(), calls=%async_computation.9 | async-start | bytes 5242880 | tf_op jit(solution)/shard_map/all_gather | solution.py:166
  20.1 458.1 %all-gather.15.cloned.1.call-start = ((), (), s32[]{:S(2)}) async-start(), calls=%async_computation.11 | async-start | bytes 2359296 | tf_op jit(solution)/shard_map/all_gather | solution.py:172
  20.7 501.4 %reduce-scatter.16.cloned.1.call-start = ((), (), s32[]{:S(2)}) async-start(), calls=%async_computation.17 | async-start | bytes 1179648 | tf_op jit(solution)/shard_map/reduce_scatter | solution.py:253
  36.0 93.8 %copy-start.14 = (f32[2048,8]{0,1:T(8,128)}, f32[2048,8]{0,1:T(8,128)S(1)}, u32[]{:S(2)}) copy-start(f32[2048,8]{0,1:T(8,128)S(1)} %get-tuple-element.435) | copy-start | bytes 196612
  153.7 4.4 copy-start.18
  158.1 49.6 %copy-start.12 = (bf16[1024,256]{1,0:T(8,128)(2,1)S(1)}, bf16[1024,256]{1,0:T(8,128)(2,1)}, u32[]{:S(2)}) copy-start(bf16[1024,256]{1,0:T(8,128)(2,1)} %all_gather.27) | copy-start | bytes 1572868
  226.2 2.5 copy-start.2
  226.2 2.5 copy-start.4
  228.7 3.2 copy-start
  235.4 3.5 copy-start.6
  235.4 9.3 copy-start.1
  238.9 5.9 copy-start.3
  250.5 2.5 copy-start.2
  250.5 2.5 copy-start.4
  252.9 3.2 copy-start
  259.7 3.5 copy-start.6
  259.7 8.7 copy-start.1
  263.1 5.3 copy-start.3
  306.2 2.5 copy-start.2
  306.2 2.5 copy-start.4
  308.6 3.2 copy-start
  315.4 3.5 copy-start.6
  315.4 8.8 copy-start.1
  318.8 5.3 copy-start.3
  329.9 2.5 copy-start.2
  329.9 2.5 copy-start.4
  332.3 3.2 copy-start
  339.0 3.5 copy-start.6
  339.0 8.7 copy-start.1
  342.5 5.2 copy-start.3
  390.8 132.9 %reduce-scatter.14.cloned.1.call-start = ((), (), s32[]{:S(2)}) async-start(), calls=%async_computation.16 | async-start | bytes 3538944 | tf_op jit(solution)/shard_map/reduce_scatter | solution.py:252
  390.9 8.0 copy-start.5
  408.0 7.9 copy-start.15
  408.0 7.9 copy-start.17
  426.1 8.4 copy-start.29
  434.5 99.5 %reduce-scatter.20.cloned.1.call-start = ((), (), s32[]{:S(2)}) async-start(), calls=%async_computation.19 | async-start | bytes 4718592 | tf_op jit(solution)/shard_map/reduce_scatter | solution.py:255
  434.6 27.4 %copy-start.32 = (bf16[2,1024,1024]{2,1,0:T(8,128)(2,1)S(1)}, bf16[2,1024,1024]{2,1,0:T(8,128)(2,1)}, u32[]{:S(2)}) copy-start(bf16[2,1024,1024]{2,1,0:T(8,128)(2,1)} %all-gather.17.cloned.1.call-done) | copy-start | bytes 12582916
  460.0 2.0 copy-start.34
  468.2 1.2 copy-start.9
  468.2 1.5 copy-start.10
  468.2 212.5 %reduce-scatter.10.cloned.1.call-start = ((), (), s32[]{:S(2)}) async-start(), calls=%async_computation.14 | async-start | bytes 10485760 | tf_op jit(solution)/shard_map/reduce_scatter | solution.py:264
  478.1 350.1 %reduce-scatter.12.cloned.1.call-start = ((), (), s32[]{:S(2)}) async-start(), calls=%async_computation.15 | async-start | bytes 10485760 | tf_op jit(solution)/shard_map/reduce_scatter | solution.py:270
  478.2 11.6 %copy-start.33 = (bf16[1024,1024]{1,0:T(8,128)(2,1)S(1)}, bf16[1024,1024]{1,0:T(8,128)(2,1)}, u32[]{:S(2)}) copy-start(bf16[1024,1024]{1,0:T(8,128)(2,1)} %all-gather.13.cloned.1.call-done) | copy-start | bytes 6291460
  489.8 6.9 copy-start.35
  496.7 7.1 copy-start.13
  496.7 479.0 %reduce-scatter.8.cloned.1.call-start = ((), (), s32[]{:S(2)}) async-start(), calls=%async_computation.12 | async-start | bytes 10485760 | tf_op jit(solution)/shard_map/reduce_scatter | solution.py:209
  508.5 523.4 %reduce-scatter.18.cloned.1.call-start = ((), (), s32[]{:S(2)}) async-start(), calls=%async_computation.18 | async-start | bytes 4718592 | tf_op jit(solution)/shard_map/reduce_scatter | solution.py:254
  519.0 1.3 copy-start.11
  519.0 309.2 %copy-start.8 = (bf16[2,256,1024]{2,1,0:T(8,128)(2,1)S(1)}, bf16[2,256,1024]{2,1,0:T(8,128)(2,1)}, u32[]{:S(2)}) copy-start(bf16[2,256,1024]{2,1,0:T(8,128)(2,1)} %param.23) | copy-start | bytes 3145732
  519.0 309.2 %copy-start.21 = (f32[2,256]{1,0:T(2,128)S(1)}, f32[2,256]{1,0:T(2,128)}, u32[]{:S(2)}) copy-start(f32[2,256]{1,0:T(2,128)} %copy-done.20) | copy-start | bytes 6148
  519.1 309.2 %copy-start.23 = (f32[1024]{0:T(1024)S(1)}, f32[1024]{0:T(1024)}, u32[]{:S(2)}) copy-start(f32[1024]{0:T(1024)} %copy-done.22) | copy-start | bytes 12292
  519.1 309.2 %copy-start.25 = (f32[1024]{0:T(1024)S(1)}, f32[1024]{0:T(1024)}, u32[]{:S(2)}) copy-start(f32[1024]{0:T(1024)} %copy-done.24) | copy-start | bytes 12292
  519.1 309.2 %copy-start.27 = (f32[2,256]{1,0:T(2,128)S(1)}, f32[2,256]{1,0:T(2,128)}, u32[]{:S(2)}) copy-start(f32[2,256]{1,0:T(2,128)} %copy-done.26) | copy-start | bytes 6148
  1021.6 10.9 %copy-start.28 = (f32[1024]{0:T(1024)}, f32[1024]{0:T(1024)S(1)}, u32[]{:S(2)}) copy-start(f32[1024]{0:T(1024)S(1)} %get-tuple-element.915) | copy-start | bytes 12292
  (6 other events, 5.3 us)
Sparse Core Ops, SparseCore 0:
  10.5 28.5 all-gather.8
  41.2 80.9 all-gather.6
  123.8 79.2 all-gather.16
  204.9 26.4 all-gather.12
  233.3 80.7 all-gather.10
  315.9 26.4 all-gather.14
  391.0 33.9 reduce-scatter.15
  434.6 44.2 reduce-scatter.13
  482.6 51.3 reduce-scatter.19
  536.2 144.4 reduce-scatter.9
  683.0 145.1 reduce-scatter.11
  830.5 145.1 reduce-scatter.7
  979.6 52.2 reduce-scatter.17
where the time goes:
time: 1050 us; the launch traced here: 1040 us
  waiting for transfers between devices  543 us (52%)
  matrix products  181 us (17%)
  local copies, waits for them, and re-layouts  158 us (15%)
  other arithmetic  70.7 us (7%)
  blocking collectives  54.7 us (5%)
  loops' own time  16.8 us (2%)
  between operations  14.9 us (1%)
    reduce_scatter x1, waiting for transfers between devices, shards(): lax.psum_scatter(grad_second.reshape(seq_count, length_all, model_width),...  148 us
    reduce_scatter x1, waiting for transfers between devices, shards(): lax.psum_scatter(grad_first.reshape(seq_count, length_all, model_width),...  145 us
    reduce_scatter x1, waiting for transfers between devices, shards(): lax.psum_scatter(branch_terms.reshape(seq_count, length_all, model_width)...  144 us
    all_gather x1, waiting for transfers between devices, shards(): lax.all_gather(first_in, 'tensor', axis=1, tiled=True)  83.2 us
    dynamic_update_slice x8, local copies, waits for them, and re-layouts, shards(): lax.map(backward_sequence, (queries, keys_all, values, grad_attended.resh...  49.7 us
    psum x1, blocking collectives, shards(): lax.psum((norm_terms[0], norm_terms[1], norm_terms[2], norm_terms[3], pad...  42.3 us
    dot_general x1, matrix products, shards(): jnp.dot(second_rows, full_up, preferred_element_type=jnp.float32) + bias_up  25.4 us
    unnamed x68, local copies, waits for them, and re-layouts  22.6 us
  transfers between devices with their start and end apart: 13, of which 7 were waited for; matrix products, arithmetic and copies ran while one was open for 38% of the time, Pallas kernels for 0%

commit v1 on v0

v1 whole, which is shorter than its diff:
```python
import math

import jax
import jax.numpy as jnp
from jax import lax
from jax.experimental import pallas as pl
from jax.experimental.pallas import tpu as pltpu
from jax.sharding import PartitionSpec as P

HEAD_DIM = 64
ROT = 16
PAIR = 2 * HEAD_DIM
ROWS = 256

EPSILON = 1e-05
BY_COLUMNS = (((1,), (1,)), ((), ()))
BY_ROWS = (((0,), (0,)), ((), ()))
F32 = jnp.float32
BF16 = jnp.bfloat16


def shifted(array, axis_name, size, shift):
    return lax.ppermute(array, axis_name, [(i, (i + shift) % size) for i in range(size)])


def swapped(array, axis_name, size, bit):
    return lax.ppermute(array, axis_name, [(i, i ^ bit) for i in range(size)])


def gather_tokens(block, axis_name, size, me):
    whole = jnp.zeros((block.shape[0], size) + block.shape[1:], block.dtype)
    pieces = [block] + [shifted(block, axis_name, size, k) for k in range(1, size)]
    for k, piece in enumerate(pieces):
        owner = lax.rem(me - k + size, size)
        whole = lax.dynamic_update_slice_in_dim(whole, piece[:, None], owner, 1)
    return whole


def scatter_tokens(parts, axis_name, size, me):
    def part_for(owner):
        return lax.dynamic_index_in_dim(parts, owner, 1, keepdims=False)

    total = part_for(me).astype(F32)
    for k in range(1, size):
        sent = part_for(lax.rem(me + k, size)).astype(BF16)
        total = total + shifted(sent, axis_name, size, k).astype(F32)
    return total


def bits_of(size):
    return [1 << i for i in range(size.bit_length() - 1)]


def gather_rows(block, axis_name, size, me, order):
    held = block
    for bit in order:
        other = swapped(held, axis_name, size, bit)
        upper = (me & bit) != 0
        held = jnp.stack([jnp.where(upper, other, held), jnp.where(upper, held, other)])
    axes = list(reversed(order))
    wanted = [axes.index(bit) for bit in reversed(bits_of(size))]
    count = len(order)
    held = held.transpose(wanted + list(range(count, held.ndim)))
    return held.reshape((size,) + block.shape)


def scatter_rows(parts, axis_name, size, me, order):
    bits = list(reversed(bits_of(size)))
    held = parts.reshape((2,) * len(bits) + parts.shape[1:])
    for bit in order:
        at = bits.index(bit)
        mine = (me // bit) % 2
        keep = lax.dynamic_index_in_dim(held, mine, at, keepdims=False)
        give = lax.dynamic_index_in_dim(held, 1 - mine, at, keepdims=False)
        held = keep + swapped(give.astype(BF16), axis_name, size, bit).astype(F32)
        bits.pop(at)
    return held


def sum_everywhere(vector, axes):
    for axis_name, size in axes:
        for bit in bits_of(size):
            vector = vector + swapped(vector, axis_name, size, bit)
    return vector


def attention_kernel(
    projected_ref, grad_ref, cos_ref, sin_ref, start_ref, out_ref, grads_ref,
    queries_t, outputs_t, keys_sum, values_sum,
):
    length = cos_ref.shape[1]
    block = min(ROWS, length)
    scale = 1.0 / math.sqrt(HEAD_DIM)
    cosine, sine = cos_ref[0], sin_ref[0]
    lanes = lax.broadcasted_iota(jnp.int32, (length, PAIR), 1)
    low = lax.rem(lanes, HEAD_DIM) < ROT // 2

    def partner(u):
        return jnp.where(low, pltpu.roll(u, PAIR - ROT // 2, 1), pltpu.roll(u, ROT // 2, 1))

    def rot(u):
        return u * cosine + partner(u) * sine

    def rot_back(u):
        return u * cosine - partner(u) * sine

    queries = (rot(projected_ref[0, 0]) * scale).astype(BF16)
    rotated = rot(projected_ref[1, 0])
    keys = rotated.astype(BF16)
    keys_t = rotated.T.astype(BF16)
    values = projected_ref[2, 0].astype(BF16)
    values_t = projected_ref[2, 0].T.astype(BF16)
    grads = grad_ref[0]

    keys_sum[...] = jnp.zeros_like(keys_sum)
    values_sum[...] = jnp.zeros_like(values_sum)
    for head in range(2):
        columns = slice(head * HEAD_DIM, (head + 1) * HEAD_DIM)
        for at in range(0, length, block):
            rows = slice(at, at + block)
            seen = at + block
            query, grad = queries[rows, columns], grads[rows, columns]
            scores = lax.dot_general(keys[:seen, columns], query, BY_COLUMNS, preferred_element_type=F32)
            key_at = lax.broadcasted_iota(jnp.int32, (seen, block), 0)
            query_at = at + lax.broadcasted_iota(jnp.int32, (seen, block), 1)
            allowed = (key_at >= start_ref[0, :, rows]) & (key_at <= query_at)
            scores = jnp.where(allowed, scores, -1e30)
            powered = jnp.exp(scores - jnp.max(scores, 0, keepdims=True))
            probabilities = powered * (1.0 / jnp.sum(powered, 0, keepdims=True))
            weights = probabilities.astype(BF16)
            outputs_t[columns, rows] = jnp.dot(
                values_t[columns, :seen], weights, preferred_element_type=F32
            )
            grad_probs = lax.dot_general(
                values[:seen, columns], grad, BY_COLUMNS, preferred_element_type=F32
            )
            inner = jnp.sum(probabilities * grad_probs, 0, keepdims=True)
            grad_scores = (probabilities * (grad_probs - inner)).astype(BF16)
            queries_t[columns, rows] = jnp.dot(
                keys_t[columns, :seen], grad_scores, preferred_element_type=F32
            )
            keys_sum[:seen, columns] += jnp.dot(grad_scores, query, preferred_element_type=F32)
            values_sum[:seen, columns] += jnp.dot(weights, grad, preferred_element_type=F32)
    out_ref[0] = outputs_t[...].T.astype(BF16)
    grads_ref[0, 0] = (rot_back(queries_t[...].T) * scale).astype(BF16)
    grads_ref[1, 0] = rot_back(keys_sum[...]).astype(BF16)
    grads_ref[2, 0] = values_sum[...].astype(BF16)


def attention(projected, grad_attended, cosine, sine, starts):
    _, count, length, width = projected.shape
    pairs = width // PAIR
    work = count * length * length * width
    return pl.pallas_call(
        attention_kernel,
        grid=(count, pairs),
        out_shape=(
            jax.ShapeDtypeStruct((count, length, width), BF16),
            jax.ShapeDtypeStruct((3, count, length, width), BF16),
        ),
        in_specs=[
            pl.BlockSpec((3, 1, length, PAIR), lambda s, h: (0, s, 0, h)),
            pl.BlockSpec((1, length, PAIR), lambda s, h: (s, 0, h)),
            pl.BlockSpec((1, length, PAIR), lambda s, h: (s, 0, 0)),
            pl.BlockSpec((1, length, PAIR), lambda s, h: (s, 0, 0)),
            pl.BlockSpec((1, 1, length), lambda s, h: (s, 0, 0)),
        ],
        out_specs=(
            pl.BlockSpec((1, length, PAIR), lambda s, h: (s, 0, h)),
            pl.BlockSpec((3, 1, length, PAIR), lambda s, h: (0, s, 0, h)),
        ),
        scratch_shapes=[
            pltpu.VMEM((PAIR, length), F32),
            pltpu.VMEM((PAIR, length), F32),
            pltpu.VMEM((length, PAIR), F32),
            pltpu.VMEM((length, PAIR), F32),
        ],
        compiler_params=pltpu.CompilerParams(vmem_limit_bytes=48 * 1024 * 1024),
        cost_estimate=pl.CostEstimate(
            flops=30 * work, bytes_accessed=24 * count * length * width,
            transcendentals=work // (2 * HEAD_DIM),
        ),
        name="attention",
    )(projected, grad_attended, cosine, sine, starts)


def make_shards(dp_size, tensor_size):
    def shards(
        hidden_in, segments, ln1_gain, ln1_bias, ln2_gain, ln2_bias, w_qkv, b_qkv,
        w_out, b_out, w_up, b_up, w_down, b_down, cotangent,
    ):
        count, own_length, width = hidden_in.shape
        length = segments.shape[1]
        rows = count * length
        dp_index, tensor_index = lax.axis_index("dp"), lax.axis_index("tensor")
        local = w_qkv.shape[2]
        local_units = w_up.shape[1]
        bits = bits_of(dp_size)
        order_a = bits[1:] + bits[:1]
        order_b = bits[:0:-1] + bits[:1]

        def gather(block):
            return gather_tokens(block, "tensor", tensor_size, tensor_index).reshape(rows, width)

        def scatter(parts):
            parts = parts.reshape(count, tensor_size, own_length, width)
            return scatter_tokens(parts, "tensor", tensor_size, tensor_index)

        hidden_rows = gather(hidden_in)
        attn_w = jnp.concatenate([w_qkv, w_out[None]], 0)
        attn_full = gather_rows(attn_w, "dp", dp_size, dp_index, order_a)
        full_qkv = attn_full[:, :3].transpose(1, 0, 2, 3).reshape(3, width, local)
        full_out = attn_full[:, 3].reshape(width, local)
        full_up = gather_rows(w_up, "dp", dp_size, dp_index, order_b).reshape(width, local_units)
        cot_rows = gather(cotangent)
        full_down = gather_rows(w_down, "dp", dp_size, dp_index, order_a).reshape(width, local_units)

        zeros = jnp.sum((segments == 0).astype(jnp.int32), -1, keepdims=True)
        ones = jnp.sum((segments == 1).astype(jnp.int32), -1, keepdims=True)
        starts = jnp.where(segments >= 1, zeros, 0) + jnp.where(segments >= 2, ones, 0)
        positions = jnp.arange(length, dtype=jnp.int32)[None] - starts
        place = jnp.arange(PAIR, dtype=jnp.int32) % HEAD_DIM
        frequency = 10000.0 ** (-(place % (ROT // 2)).astype(F32) * (2.0 / ROT))
        angles = positions.astype(F32)[..., None] * frequency
        cosine = jnp.where(place < ROT, jnp.cos(angles), 1.0)
        sines = jnp.sin(angles)
        sine = jnp.where(place < ROT // 2, -sines, jnp.where(place < ROT, sines, 0.0))

        def layer_normed(hidden):
            centred = hidden - jnp.mean(hidden, -1, keepdims=True)
            scaling = lax.rsqrt(jnp.mean(centred * centred, -1, keepdims=True) + EPSILON)
            return centred * scaling, scaling

        normed, _ = layer_normed(hidden_rows.astype(F32))
        first = (normed * ln1_gain + ln1_bias).astype(BF16)
        second = (normed * ln2_gain + ln2_bias).astype(BF16)
        bias_qkv = lax.dynamic_slice_in_dim(b_qkv, tensor_index * local, local, 1)
        bias_up = lax.dynamic_slice_in_dim(b_up, tensor_index * local_units, local_units, 0)

        projected = (
            jnp.einsum("rd,cde->cre", first, full_qkv, preferred_element_type=F32)
            + bias_qkv[:, None, :]
        )
        grad_attended = jnp.dot(cot_rows, full_out, preferred_element_type=F32).astype(BF16)
        attended, grad_projected = attention(
            projected.reshape(3, count, length, local),
            grad_attended.reshape(count, length, local),
            cosine, sine, starts[:, None, :],
        )
        attended = attended.reshape(rows, local)
        grad_projected = grad_projected.reshape(3, rows, local)

        units = jnp.dot(second, full_up, preferred_element_type=F32) + bias_up
        cumulative = 0.5 * (1.0 + lax.erf(units * (1.0 / math.sqrt(2.0))))
        density = jnp.exp(-0.5 * units * units) * (1.0 / math.sqrt(2.0 * math.pi))
        activated = (units * cumulative).astype(BF16)
        slope = cumulative + units * density
        grad_units = (jnp.dot(cot_rows, full_down, preferred_element_type=F32) * slope).astype(BF16)

        branch = lax.dot_general(attended, full_out, BY_COLUMNS, preferred_element_type=F32)
        branch = branch + lax.dot_general(activated, full_down, BY_COLUMNS, preferred_element_type=F32)
        hidden = hidden_in.astype(F32)
        block_out = (hidden + scatter(branch) + b_out + b_down).astype(BF16)

        grad_first = jnp.einsum("cre,cde->rd", grad_projected, full_qkv, preferred_element_type=F32)
        grad_second = lax.dot_general(grad_units, full_up, BY_COLUMNS, preferred_element_type=F32)
        norm_terms = [
            jnp.sum(grad_first * normed, 0), jnp.sum(grad_first, 0),
            jnp.sum(grad_second * normed, 0), jnp.sum(grad_second, 0),
        ]
        e = scatter(grad_first * ln1_gain + grad_second * ln2_gain)
        own_normed, own_scaling = layer_normed(hidden)
        grad_in = cotangent.astype(F32) + own_scaling * (
            e
            - jnp.mean(e, -1, keepdims=True)
            - own_normed * jnp.mean(e * own_normed, -1, keepdims=True)
        )

        def to_owners(part, order):
            split = part.reshape((dp_size, part.shape[0] // dp_size) + part.shape[1:])
            return scatter_rows(split, "dp", dp_size, dp_index, bits[:1] + order)

        xy, yx = bits[1:], bits[:0:-1]
        grad_w_down = to_owners(lax.dot_general(cot_rows, activated, BY_ROWS, preferred_element_type=F32), xy)
        grad_w_out = to_owners(lax.dot_general(cot_rows, attended, BY_ROWS, preferred_element_type=F32), xy)
        grad_w_up = to_owners(lax.dot_general(second, grad_units, BY_ROWS, preferred_element_type=F32), yx)
        grad_w_qkv = jnp.stack([
            to_owners(lax.dot_general(first, grad_projected[c], BY_ROWS, preferred_element_type=F32), yx if c else xy)
            for c in range(3)
        ])

        padded_qkv = lax.dynamic_update_slice_in_dim(
            jnp.zeros((3, width), F32), jnp.sum(grad_projected, 1, dtype=F32), tensor_index * local, 1
        )
        padded_up = lax.dynamic_update_slice_in_dim(
            jnp.zeros(b_up.shape, F32), jnp.sum(grad_units, 0, dtype=F32), tensor_index * local_units, 0
        )
        cot_sums = jnp.sum(cotangent, (0, 1), dtype=F32)
        vector = jnp.concatenate(norm_terms + [padded_qkv.reshape(-1), cot_sums, padded_up])
        vector = vector.reshape(-1, 128)
        vector = sum_everywhere(vector, (("tensor", tensor_size), ("dp", dp_size))).reshape(-1)
        g1, b1, g2, b2, qkv, cot_sum, up = jnp.split(
            vector, [width, 2 * width, 3 * width, 4 * width, 7 * width, 8 * width]
        )
        return (
            block_out, grad_in.astype(BF16), g1, b1, g2, b2, grad_w_qkv, qkv.reshape(3, width),
            grad_w_out, cot_sum, grad_w_up, up, grad_w_down, cot_sum,
        )

    return shards


def solution(mesh):
    tokens = P("dp", "tensor", None)
    weight = P("dp", "tensor")
    stacked = P(None, "dp", "tensor")
    in_specs = (
        tokens, P("dp", None), P(), P(), P(), P(), stacked, P(),
        weight, P(), weight, P(), weight, P(), tokens,
    )
    out_specs = (
        tokens, tokens, P(), P(), P(), P(), stacked, P(),
        weight, P(), weight, P(), weight, P(),
    )
    shards = make_shards(mesh.shape["dp"], mesh.shape["tensor"])
    return jax.shard_map(shards, mesh=mesh, in_specs=in_specs, out_specs=out_specs, check_vma=False)
```

time: 1050 us -> 562 us (0.54)
  waiting for transfers between devices: 543 us -> 239 us
  matrix products: 181 us -> 79.8 us
  local copies, waits for them, and re-layouts: 158 us -> 63.8 us
  starting transfers between devices: 0.78 us -> 72.1 us
  blocking collectives: 54.7 us -> 0 us
  Pallas kernels: 0 us -> 46 us
  other arithmetic: 70.7 us -> 51.6 us
  loops' own time: 16.8 us -> 0 us
  between operations: 14.9 us -> 2.15 us
    reduce_scatter x7 -> x0, waiting for transfers between devices: 455 us -> none  [the longest x1 148 us: shards(): lax.psum_scatter(grad_second.reshape(seq_count, length_all, model_width),...]
    ppermute x0 -> x44, waiting for transfers between devices: none -> 239 us  [the longest x12 174 us: shifted(): lax.ppermute(array, axis_name, [(i, (i + shift) % size) for i in range(si...]
    dot_general x40 -> x14, matrix products: 181 us -> 79.8 us  [the longest x1 13.6 us: shards(): lax.dot_general(grad_units, full_up, BY_COLUMNS, preferred_element_type=F32)]
    all_gather x6 -> x0, waiting for transfers between devices: 85 us -> none  [the longest x1 83.2 us: shards(): lax.all_gather(first_in, 'tensor', axis=1, tiled=True)]
    ppermute x0 -> x44, starting transfers between devices: none -> 72.1 us  [the longest x12 42.3 us: shifted(): lax.ppermute(array, axis_name, [(i, (i + shift) % size) for i in range(si...]
    pallas_call x0 -> x1, Pallas kernels: none -> 46 us  [attention(): pl.pallas_call(attention_kernel, grid=(count, pairs), out_shape=(jax.Shap...]
    dynamic_update_slice x14 -> x9, local copies, waits for them, and re-layouts: 52.7 us -> 8.61 us  [the longest x7 8.3 us: gather_tokens(): whole = lax.dynamic_update_slice_in_dim(whole, piece[:, None], owner, 1)]
    psum x1 -> x0, blocking collectives: 42.3 us -> none  [shards(): lax.psum((norm_terms[0], norm_terms[1], norm_terms[2], norm_terms[3], pad...]
  transfers between devices with their start and end apart: 13 -> 44, of which waited for: 7 -> 23; matrix products, arithmetic and copies ran while one was open for 38% -> 27% of each run, Pallas kernels for 0% -> 8%
where the time goes in v1:
time: 562 us; the launch traced here: 555 us
  waiting for transfers between devices  239 us (43%)
  matrix products  79.8 us (14%)
  starting transfers between devices  72.1 us (13%)
  local copies, waits for them, and re-layouts  63.8 us (11%)
  other arithmetic  51.6 us (9%)
  Pallas kernels  46 us (8%)
    ppermute x12, waiting for transfers between devices, shifted(): lax.ppermute(array, axis_name, [(i, (i + shift) % size) for i in range(si...  174 us
    ppermute x32, waiting for transfers between devices, swapped(): return lax.ppermute(array, axis_name, [(i, i ^ bit) for i in range(size)])  65.6 us
    pallas_call x1, Pallas kernels, attention(): pl.pallas_call(attention_kernel, grid=(count, pairs), out_shape=(jax.Shap...  46 us
    ppermute x12, starting transfers between devices, shifted(): lax.ppermute(array, axis_name, [(i, (i + shift) % size) for i in range(si...  42.3 us
    ppermute x32, starting transfers between devices, swapped(): return lax.ppermute(array, axis_name, [(i, i ^ bit) for i in range(size)])  29.8 us
    dot_general x1, matrix products, shards(): lax.dot_general(grad_units, full_up, BY_COLUMNS, preferred_element_type=F32)  13.6 us
  transfers between devices with their start and end apart: 44, of which 23 were waited for; matrix products, arithmetic and copies ran while one was open for 27% of the time, Pallas kernels for 8%

profile of v1, /device:TPU:0, one launch (start us, length us, event | category | flops | bytes accessed | tf_op | source)
XLA Modules:
  0.0 555.0 jit_solution(14279864552342866774)
XLA Ops:
  0.7 3.1 collective-permute-start.6
  3.7 2.6 collective-permute-start.7
  8.7 1.6 collective-permute-start
  13.3 1.6 fusion.20
  22.4 2.5 broadcast.174.clone
  27.4 3.8 fusion.31
  35.2 3.4 collective-permute-done.12
  39.2 6.4 %collective-permute-done.1 = bf16[2,4,128,256]{3,2,1,0:T(8,128)(2,1)S(1)} collective-permute-done((bf16[2,4,128,256]{3,2,1,0:T(8,128)(2,1)S(1)}, bf16[2,4,128,256]{3,2,1,0:T(8,128)(2,1)S(1)}, u32[]{:S(2)}, u32[]{:S(2)}) %collective-permute-start.1) | collective-permute-done | bytes 524320 | tf_op jit(solution)/shard_map/ppermute | solution.py:27
  47.4 2.6 collective-permute-done.10
  50.8 6.0 %collective-permute-done.13 = bf16[2,128,1024]{2,1,0:T(8,128)(2,1)S(1)} collective-permute-done((bf16[2,128,1024]{2,1,0:T(8,128)(2,1)S(1)}, bf16[2,128,1024]{2,1,0:T(8,128)(2,1)S(1)}, u32[]{:S(2)}, u32[]{:S(2)}) %collective-permute-start.13) | collective-permute-done | bytes 524320 | tf_op jit(solution)/shard_map/ppermute | solution.py:27
  59.7 2.8 collective-permute-start.5
  62.4 2.3 bitcast_dynamic-update-slice_fusion.2
  64.7 32.8 %collective-permute-done.3 = bf16[2,256,1024]{2,1,0:T(8,128)(2,1)S(1)} collective-permute-done((bf16[2,256,1024]{2,1,0:T(8,128)(2,1)S(1)}, bf16[2,256,1024]{2,1,0:T(8,128)(2,1)S(1)}, u32[]{:S(2)}, u32[]{:S(2)}) %collective-permute-start.3) | collective-permute-done | bytes 1048608 | tf_op jit(solution)/shard_map/ppermute | solution.py:23
  98.3 2.2 bitcast_dynamic-update-slice_fusion.1
  100.5 63.6 %collective-permute-done.4 = bf16[2,256,1024]{2,1,0:T(8,128)(2,1)S(1)} collective-permute-done((bf16[2,256,1024]{2,1,0:T(8,128)(2,1)S(1)}, bf16[2,256,1024]{2,1,0:T(8,128)(2,1)S(1)}, u32[]{:S(2)}, u32[]{:S(2)}) %collective-permute-start.4) | collective-permute-done | bytes 1048608 | tf_op jit(solution)/shard_map/ppermute | solution.py:23
  164.3 2.4 bitcast_dynamic-update-slice_fusion
  168.7 6.5 %copy.79 = bf16[2048,1024]{0,1:T(8,128)(2,1)} copy(bf16[2048,1024]{1,0:T(8,128)(2,1)} %bitcast.31) | data formatting | bytes 8388608 | tf_op jit(solution)/shard_map/reshape | solution.py:203
  175.2 6.2 %add_convert_fusion.3 = (bf16[2,4,256,1024]{3,2,1,0:T(8,128)(2,1)}, bf16[2,4,256,1024]{3,2,1,0:T(8,128)(2,1)}) fusion(bf16[2,4,256,1024]{3,2,1,0:T(8,128)(2,1)} %copy-done, f32[1024]{0:T(1024)S(1)} %convert_element_type.319, f32[1024]{0:T(1024)S(1)} %convert_element_type.318, f32[2,4,256]{2,1,0:T(4,128)S(1)} %get-tuple-element.76, ...), kind=kLoop, calls=%fused_computation.21 | loop fusion | flops 18874368 | bytes 12615680 | tf_op jit(solution)/shard_map/convert_element_type | solution.py:235
  184.4 3.0 copy.53
  187.4 3.7 reshape.243
  191.1 8.8 %add_bitcast_fusion = f32[3,2048,256]{1,2,0:T(8,128)} fusion(bf16[3,1024,256]{1,2,0:T(8,128)(2,1)} %reshape.243, bf16[2048,1024,1]{1,0,2:T(8,128)(2,1)} %bitcast.363, f32[3,256]{1,0:T(4,128)S(1)} %fusion.63), kind=kOutput, calls=%fused_computation.25 | convolution fusion | flops 3222798336 | bytes 12061696 | tf_op jit(solution)/shard_map/rd,cde->cre/dot_general | solution.py:241
  199.9 6.6 %copy.58 = f32[3,2048,256]{2,1,0:T(8,128)} copy(f32[3,2048,256]{1,2,0:T(8,128)} %add_bitcast_fusion) | data formatting | bytes 12582912 | tf_op jit(solution)/shard_map/add | solution.py:241
  206.5 3.5 convolution_convert_fusion
  211.9 46.0 %attention.1 = (bf16[2,1024,256]{2,1,0:T(8,128)(2,1)S(1)}, bf16[3,2,1024,256]{3,2,1,0:T(8,128)(2,1)}) custom-call(f32[3,2,1024,256]{3,2,1,0:T(8,128)} %bitcast.361, bf16[2,1024,256]{2,1,0:T(8,128)(2,1)S(1)} %bitcast.355, f32[2,1024,128]{2,1,0:T(8,128)S(1)} %get-tuple-element.72.cos_ref, f32[2,1024,128]{2,1,0:T(8,128)S(1)} %get-tuple-element.71.sin_ref, ...), custom_call_target="tpu_custom_call" | custom-call | flops 16106127360 | bytes 12582912 | tf_op jit(solution)/shard_map/attention/pallas_call | solution.py:154
  257.9 2.5 convert_reduce_fusion.2
  260.8 1.7 fusion.75
  262.5 5.6 %fusion.77 = f32[2048,1024,1]{1,0,2:T(8,128)} fusion(bf16[3,2048,256]{2,1,0:T(8,128)(2,1)S(1)} %bitcast.358, bf16[3,1024,256]{1,2,0:T(8,128)(2,1)S(1)} %copy-done.30), kind=kOutput, calls=%fused_computation.217 | convolution fusion | flops 3221225472 | bytes 13107200 | tf_op jit(solution)/shard_map/cre,cde->rd/dot_general | solution.py:265
  270.6 10.8 %multiply_convert_fusion = (bf16[2048,1024]{1,0:T(8,128)(2,1)}, f32[2048,1024]{1,0:T(8,128)S(1)}) fusion(f32[1024]{0:T(1024)S(1)} %dynamic-slice_convert_fusion.16, bf16[2048,1024]{1,0:T(8,128)(2,1)S(1)} %bitcast.362, bf16[1024,1024]{1,0:T(8,128)(2,1)S(1)} %bitcast.378), kind=kOutput, calls=%fused_computation.18 | convolution fusion | flops 4307550208 | bytes 18878464 | tf_op jit(solution)/shard_map/dot_general | solution.py:253
  281.4 10.1 %convert_reduce_fusion = (f32[1024]{0:T(1024)S(1)}, bf16[2048,1024]{1,0:T(8,128)(2,1)}) fusion(f32[2048,1024]{1,0:T(8,128)S(1)} %get-tuple-element.78, f32[1024]{0:T(1024)S(1)} %dynamic-slice_convert_fusion.16, bf16[2048,1024]{1,0:T(8,128)(2,1)} %bitcast.31, bf16[1024,1024]{1,0:T(8,128)(2,1)S(1)} %bitcast.376), kind=kOutput, calls=%fused_computation.16 | convolution fusion | flops 4322229248 | bytes 18882560 | tf_op jit(solution)/shard_map/dot_general | solution.py:258
  291.6 13.6 %fusion.71 = (f32[1024]{0:T(1024)S(1)}, f32[1024]{0:T(1024)S(1)}, f32[2048,1024]{1,0:T(8,128)S(1)}, f32[1024]{0:T(1024)S(1)}, f32[1024]{0:T(1024)S(1)}, /*index=...) fusion(f32[2048]{0:T(1024)S(1)} %bitcast.386, f32[2048]{0:T(1024)S(1)} %bitcast.387, ...), kind=kOutput, calls=%fused_computation.213 | convolution fusion | flops 4332711936 | bytes 35700736 | tf_op jit(solution)/shard_map/dot_general | solution.py:266
  305.2 1.8 fusion.38
  307.0 24.0 %collective-permute-start.20 = (bf16[2,256,1024]{2,1,0:T(8,128)(2,1)}, bf16[2,256,1024]{2,1,0:T(8,128)(2,1)}, u32[]{:S(2)}, u32[]{:S(2)}) collective-permute-start(bf16[2,256,1024]{2,1,0:T(8,128)(2,1)} %get-tuple-element.34), channel_id=1, source_target_pairs={{0,3},{1,0},{2,1},{3,2},{4,7},{5,4},{6,5},{7,6},{8,11},{9,8},{10,9... | collective-permute-start | bytes 3145736 | tf_op jit(solution)/shard_map/ppermute | solution.py:23
  331.5 4.6 fusion.76
  337.5 3.3 copy-done.4
  342.3 6.7 %copy.89 = bf16[1024,2048]{1,0:T(8,128)(2,1)} copy(bf16[1024,2048]{0,1:T(8,128)(2,1)} %bitcast.367) | data formatting | bytes 8388608 | tf_op jit(solution)/shard_map/dot_general | solution.py:288
  349.0 3.9 fusion.80
  359.7 6.1 %fusion.9 = f32[2,2,2,128,1024]{4,3,2,1,0:T(8,128)} fusion(bf16[2,2,2,128,2048]{4,3,2,1,0:T(8,128)(2,1)S(1)} %bitcast.364, bf16[2048,1024]{1,0:T(8,128)(2,1)S(1)} %copy-done.54), kind=kOutput, calls=%fused_computation.27 | convolution fusion | flops 4294967296 | bytes 12582912 | tf_op jit(solution)/shard_map/dot_general | solution.py:284
  368.0 6.5 %copy.88 = bf16[1024,2048]{1,0:T(8,128)(2,1)} copy(bf16[1024,2048]{0,1:T(8,128)(2,1)} %bitcast.366) | data formatting | bytes 8388608 | tf_op jit(solution)/shard_map/dot_general | solution.py:286
  374.5 7.6 %fusion.11 = f32[2,2,2,128,1024]{4,3,2,1,0:T(8,128)S(1)} fusion(bf16[2,2,2,128,2048]{4,3,2,1,0:T(8,128)(2,1)} %bitcast.371, bf16[2048,1024]{1,0:T(8,128)(2,1)} %get-tuple-element.80), kind=kOutput, calls=%fused_computation.29 | convolution fusion | flops 4294967296 | bytes 12582912 | tf_op jit(solution)/shard_map/dot_general | solution.py:286
  384.8 5.0 collective-permute-start.17
  389.8 1.6 collective-permute-start.33
  391.5 3.6 collective-permute-done.33
  396.7 3.4 collective-permute-done.30
  401.6 3.5 collective-permute-done.27
  406.6 4.1 collective-permute-done.36
  412.3 2.7 collective-permute-done.34
  416.5 2.8 collective-permute-done.31
  420.7 2.7 collective-permute-done.28
  425.0 2.7 collective-permute-done.37
  428.0 1.7 collective-permute-start.15
  430.9 3.5 fusion.72
  434.4 15.3 %collective-permute-done.17 = bf16[2,256,1024]{2,1,0:T(8,128)(2,1)S(1)} collective-permute-done((bf16[2,256,1024]{2,1,0:T(8,128)(2,1)S(1)}, bf16[2,256,1024]{2,1,0:T(8,128)(2,1)S(1)}, u32[]{:S(2)}, u32[]{:S(2)}) %collective-permute-start.17) | collective-permute-done | bytes 1048608 | tf_op jit(solution)/shard_map/ppermute | solution.py:23
  449.7 62.1 %collective-permute-done.16 = bf16[2,256,1024]{2,1,0:T(8,128)(2,1)S(1)} collective-permute-done((bf16[2,256,1024]{2,1,0:T(8,128)(2,1)S(1)}, bf16[2,256,1024]{2,1,0:T(8,128)(2,1)S(1)}, u32[]{:S(2)}, u32[]{:S(2)}) %collective-permute-start.16) | collective-permute-done | bytes 1048608 | tf_op jit(solution)/shard_map/ppermute | solution.py:23
  511.8 4.1 convert_reduce_fusion.4
  517.1 3.0 collective-permute-done.21
  520.1 2.4 collective-permute-start.22
  522.7 2.7 collective-permute-done.22
  525.6 1.6 collective-permute-start.39
  527.2 1.6 collective-permute-start.24
  529.1 2.3 collective-permute-done.24
  532.5 1.6 collective-permute-start.42
  534.1 6.9 %collective-permute-done.25 = f32[96,128]{1,0:T(8,128)S(1)} collective-permute-done((f32[96,128]{1,0:T(8,128)S(1)}, f32[96,128]{1,0:T(8,128)S(1)}, u32[]{:S(2)}, u32[]{:S(2)}) %collective-permute-start.25) | collective-permute-done | bytes 49184 | tf_op jit(solution)/shard_map/ppermute | solution.py:27
  543.4 3.1 collective-permute-done.42
  548.7 2.4 collective-permute-done.40
  (278 shorter events, 73.9 us)
Async XLA Ops:
  0.6 24.3 %copy-start.21 = (bf16[2,256,1024]{2,1,0:T(8,128)(2,1)S(1)}, bf16[2,256,1024]{2,1,0:T(8,128)(2,1)}, u32[]{:S(2)}) copy-start(bf16[2,256,1024]{2,1,0:T(8,128)(2,1)} %param.29) | copy-start | bytes 3145732
  0.7 59.0 %collective-permute-start.6 = (bf16[2,256,1024]{2,1,0:T(8,128)(2,1)}, bf16[2,256,1024]{2,1,0:T(8,128)(2,1)}, u32[]{:S(2)}, u32[]{:S(2)}) collective-permute-start(bf16[2,256,1024]{2,1,0:T(8,128)(2,1)} %param.29), channel_id=1, source_target_pairs={{0,1},{1,2},{2,3},{3,0},{4,5},{5,6},{6,7},{7,4},{8,9},{9,10},{10,1... | collective-permute-start | bytes 3145736 | tf_op jit(solution)/shard_map/ppermute | solution.py:23
  3.7 94.0 %collective-permute-start.7 = (bf16[2,256,1024]{2,1,0:T(8,128)(2,1)}, bf16[2,256,1024]{2,1,0:T(8,128)(2,1)}, u32[]{:S(2)}, u32[]{:S(2)}) collective-permute-start(bf16[2,256,1024]{2,1,0:T(8,128)(2,1)} %param.29), channel_id=1, source_target_pairs={{0,2},{1,3},{2,0},{3,1},{4,6},{5,7},{6,4},{7,5},{8,10},{9,11},{10,... | collective-permute-start | bytes 3145736 | tf_op jit(solution)/shard_map/ppermute | solution.py:23
  6.3 157.9 %collective-permute-start.8 = (bf16[2,256,1024]{2,1,0:T(8,128)(2,1)}, bf16[2,256,1024]{2,1,0:T(8,128)(2,1)}, u32[]{:S(2)}, u32[]{:S(2)}) collective-permute-start(bf16[2,256,1024]{2,1,0:T(8,128)(2,1)} %param.29), channel_id=1, source_target_pairs={{0,3},{1,0},{2,1},{3,2},{4,7},{5,4},{6,5},{7,6},{8,11},{9,8},{10,9... | collective-permute-start | bytes 3145736 | tf_op jit(solution)/shard_map/ppermute | solution.py:23
  8.7 23.2 %collective-permute-start = (bf16[4,128,256]{2,1,0:T(8,128)(2,1)S(1)}, bf16[4,128,256]{2,1,0:T(8,128)(2,1)}, u32[]{:S(2)}, u32[]{:S(2)}) collective-permute-start(bf16[4,128,256]{2,1,0:T(8,128)(2,1)S(1)} %pad_maximum_fusion.9), channel_id=1, source_target_pairs={{0,8},{4,12},{8,0},{12,4},{16,24},{20,28},{24,16},{28,20},{1,9},{5... | collective-permute-start | bytes 786440 | tf_op jit(solution)/shard_map/ppermute | solution.py:27
  10.2 23.3 %collective-permute-start.9 = (bf16[128,1024]{1,0:T(8,128)(2,1)}, bf16[128,1024]{1,0:T(8,128)(2,1)}, u32[]{:S(2)}, u32[]{:S(2)}) collective-permute-start(bf16[128,1024]{1,0:T(8,128)(2,1)} %param.25), channel_id=1, source_target_pairs={{0,16},{4,20},{8,24},{12,28},{16,0},{20,4},{24,8},{28,12},{1,17},{... | collective-permute-start | bytes 786440 | tf_op jit(solution)/shard_map/ppermute | solution.py:27
  31.9 6.7 %collective-permute-start.12 = (bf16[128,1024]{1,0:T(8,128)(2,1)S(1)}, bf16[128,1024]{1,0:T(8,128)(2,1)S(1)}, u32[]{:S(2)}, u32[]{:S(2)}) collective-permute-start(bf16[128,1024]{1,0:T(8,128)(2,1)S(1)} %copy-done.45), channel_id=1, source_target_pairs={{0,8},{4,12},{8,0},{12,4},{16,24},{20,28},{24,16},{28,20},{1,9},{5... | collective-permute-start | bytes 786440 | tf_op jit(solution)/shard_map/ppermute | solution.py:27
  33.6 12.0 %collective-permute-start.1 = (bf16[2,4,128,256]{3,2,1,0:T(8,128)(2,1)S(1)}, bf16[2,4,128,256]{3,2,1,0:T(8,128)(2,1)S(1)}, u32[]{:S(2)}, u32[]{:S(2)}) collective-permute-start(bf16[2,4,128,256]{3,2,1,0:T(8,128)(2,1)S(1)} %pad_maximum_fusion.5), channel_id=1, source_target_pairs={{0,16},{4,20},{8,24},{12,28},{16,0},{20,4},{24,8},{28,12},{1,17},{... | collective-permute-start | bytes 1572872 | tf_op jit(solution)/shard_map/ppermute | solution.py:27
  38.6 11.4 %collective-permute-start.10 = (bf16[2,128,1024]{2,1,0:T(8,128)(2,1)S(1)}, bf16[2,128,1024]{2,1,0:T(8,128)(2,1)S(1)}, u32[]{:S(2)}, u32[]{:S(2)}) collective-permute-start(bf16[2,128,1024]{2,1,0:T(8,128)(2,1)S(1)} %pad_maximum_fusion.6), channel_id=1, source_target_pairs={{0,8},{4,12},{8,0},{12,4},{16,24},{20,28},{24,16},{28,20},{1,9},{5... | collective-permute-start | bytes 1572872 | tf_op jit(solution)/shard_map/ppermute | solution.py:27
  45.6 11.2 %collective-permute-start.13 = (bf16[2,128,1024]{2,1,0:T(8,128)(2,1)S(1)}, bf16[2,128,1024]{2,1,0:T(8,128)(2,1)S(1)}, u32[]{:S(2)}, u32[]{:S(2)}) collective-permute-start(bf16[2,128,1024]{2,1,0:T(8,128)(2,1)S(1)} %pad_maximum_fusion.7), channel_id=1, source_target_pairs={{0,16},{4,20},{8,24},{12,28},{16,0},{20,4},{24,8},{28,12},{1,17},{... | collective-permute-start | bytes 1572872 | tf_op jit(solution)/shard_map/ppermute | solution.py:27
  50.1 47.5 %collective-permute-start.3 = (bf16[2,256,1024]{2,1,0:T(8,128)(2,1)S(1)}, bf16[2,256,1024]{2,1,0:T(8,128)(2,1)S(1)}, u32[]{:S(2)}, u32[]{:S(2)}) collective-permute-start(bf16[2,256,1024]{2,1,0:T(8,128)(2,1)S(1)} %copy-done.2), channel_id=1, source_target_pairs={{0,1},{1,2},{2,3},{3,0},{4,5},{5,6},{6,7},{7,4},{8,9},{9,10},{10,1... | collective-permute-start | bytes 3145736 | tf_op jit(solution)/shard_map/ppermute | solution.py:23
  50.8 13.9 %copy-start.6 = (bf16[1,2,128,1024]{3,2,0,1:T(8,128)(2,1)}, bf16[1,2,128,1024]{3,2,0,1:T(8,128)(2,1)S(1)}, u32[]{:S(2)}) copy-start(bf16[1,2,128,1024]{3,2,0,1:T(8,128)(2,1)S(1)} %get-tuple-element.58) | copy-start | bytes 1572868
  50.8 13.9 %copy-start.8 = (bf16[1,2,128,1024]{3,2,0,1:T(8,128)(2,1)}, bf16[1,2,128,1024]{3,2,0,1:T(8,128)(2,1)S(1)}, u32[]{:S(2)}) copy-start(bf16[1,2,128,1024]{3,2,0,1:T(8,128)(2,1)S(1)} %get-tuple-element.59) | copy-start | bytes 1572868
  56.8 107.3 %collective-permute-start.4 = (bf16[2,256,1024]{2,1,0:T(8,128)(2,1)S(1)}, bf16[2,256,1024]{2,1,0:T(8,128)(2,1)S(1)}, u32[]{:S(2)}, u32[]{:S(2)}) collective-permute-start(bf16[2,256,1024]{2,1,0:T(8,128)(2,1)S(1)} %copy-done.2), channel_id=1, source_target_pairs={{0,2},{1,3},{2,0},{3,1},{4,6},{5,7},{6,4},{7,5},{8,10},{9,11},{10,... | collective-permute-start | bytes 3145736 | tf_op jit(solution)/shard_map/ppermute | solution.py:23
  57.4 40.3 %copy-start.14 = (bf16[1,2,128,1024]{3,2,0,1:T(8,128)(2,1)}, bf16[1,2,128,1024]{3,2,0,1:T(8,128)(2,1)S(1)}, u32[]{:S(2)}) copy-start(bf16[1,2,128,1024]{3,2,0,1:T(8,128)(2,1)S(1)} %get-tuple-element.56) | copy-start | bytes 1572868
  57.4 40.3 %copy-start.16 = (bf16[1,2,128,1024]{3,2,0,1:T(8,128)(2,1)}, bf16[1,2,128,1024]{3,2,0,1:T(8,128)(2,1)S(1)}, u32[]{:S(2)}) copy-start(bf16[1,2,128,1024]{3,2,0,1:T(8,128)(2,1)S(1)} %get-tuple-element.57) | copy-start | bytes 1572868
  59.7 104.6 %collective-permute-start.5 = (bf16[2,256,1024]{2,1,0:T(8,128)(2,1)S(1)}, bf16[2,256,1024]{2,1,0:T(8,128)(2,1)S(1)}, u32[]{:S(2)}, u32[]{:S(2)}) collective-permute-start(bf16[2,256,1024]{2,1,0:T(8,128)(2,1)S(1)} %copy-done.2), channel_id=1, source_target_pairs={{0,3},{1,0},{2,1},{3,2},{4,7},{5,4},{6,5},{7,6},{8,11},{9,8},{10,9... | collective-permute-start | bytes 3145736 | tf_op jit(solution)/shard_map/ppermute | solution.py:23
  97.6 83.9 %collective-permute-start.2 = (bf16[2,2,4,128,256]{4,3,2,1,0:T(8,128)(2,1)}, bf16[2,2,4,128,256]{4,3,2,1,0:T(8,128)(2,1)}, u32[]{:S(2)}, u32[]{:S(2)}) collective-permute-start(bf16[2,2,4,128,256]{4,3,2,1,0:T(8,128)(2,1)} %pad_maximum_fusion.2), channel_id=1, source_target_pairs={{0,4},{4,0},{8,12},{12,8},{16,20},{20,16},{24,28},{28,24},{1,5},{5... | collective-permute-start | bytes 3145736 | tf_op jit(solution)/shard_map/ppermute | solution.py:27
  97.7 170.4 %collective-permute-start.11 = (bf16[2,2,128,1024]{3,2,0,1:T(8,128)(2,1)}, bf16[2,2,128,1024]{3,2,0,1:T(8,128)(2,1)}, u32[]{:S(2)}, u32[]{:S(2)}) collective-permute-start(bf16[2,2,128,1024]{3,2,0,1:T(8,128)(2,1)} %pad_maximum_fusion.3), channel_id=1, source_target_pairs={{0,4},{4,0},{8,12},{12,8},{16,20},{20,16},{24,28},{28,24},{1,5},{5... | collective-permute-start | bytes 3145736 | tf_op jit(solution)/shard_map/ppermute | solution.py:27
  164.1 45.9 %collective-permute-start.14 = (bf16[2,2,128,1024]{3,2,0,1:T(8,128)(2,1)}, bf16[2,2,128,1024]{3,2,0,1:T(8,128)(2,1)}, u32[]{:S(2)}, u32[]{:S(2)}) collective-permute-start(bf16[2,2,128,1024]{3,2,0,1:T(8,128)(2,1)} %pad_maximum_fusion.4), channel_id=1, source_target_pairs={{0,4},{4,0},{8,12},{12,8},{16,20},{20,16},{24,28},{28,24},{1,5},{5... | collective-permute-start | bytes 3145736 | tf_op jit(solution)/shard_map/ppermute | solution.py:27
  184.4 22.1 %copy-start.25 = (bf16[8,1,128,256]{3,2,1,0:T(8,128)(2,1)}, bf16[8,1,128,256]{3,2,1,0:T(8,128)(2,1)S(1)}, u32[]{:S(2)}) copy-start(bf16[8,1,128,256]{3,2,1,0:T(8,128)(2,1)S(1)} %slice.31) | copy-start | bytes 1572868
  211.9 69.5 %copy-start.27 = (bf16[2,2,2,128,1024]{4,3,2,1,0:T(8,128)(2,1)}, bf16[2,2,2,128,1024]{4,3,2,1,0:T(8,128)(2,1)S(1)}, u32[]{:S(2)}) copy-start(bf16[2,2,2,128,1024]{4,3,2,1,0:T(8,128)(2,1)S(1)} %copy.66) | copy-start | bytes 6291460
  269.9 11.6 %copy-start.29 = (bf16[2,2,2,128,1024]{4,3,0,1,2:T(8,128)(2,1)}, bf16[2,2,2,128,1024]{4,3,0,1,2:T(8,128)(2,1)S(1)}, u32[]{:S(2)}) copy-start(bf16[2,2,2,128,1024]{4,3,0,1,2:T(8,128)(2,1)S(1)} %pad_maximum_fusion.1) | copy-start | bytes 6291460
  281.4 10.1 %copy-start.1 = (bf16[2,4,256,1024]{3,2,1,0:T(8,128)(2,1)S(1)}, bf16[2,4,256,1024]{3,2,1,0:T(8,128)(2,1)}, u32[]{:S(2)}) copy-start(bf16[2,4,256,1024]{3,2,1,0:T(8,128)(2,1)} %copy-done) | copy-start | bytes 12582916
  305.2 31.0 %copy-start.23 = (f32[2048,1024]{1,0:T(8,128)}, f32[2048,1024]{1,0:T(8,128)S(1)}, u32[]{:S(2)}) copy-start(f32[2048,1024]{1,0:T(8,128)S(1)} %get-tuple-element.29) | copy-start | bytes 25165828
  305.2 26.4 %copy-start.28 = (bf16[2,2,2,128,1024]{4,3,2,1,0:T(8,128)(2,1)S(1)}, bf16[2,2,2,128,1024]{4,3,2,1,0:T(8,128)(2,1)}, u32[]{:S(2)}) copy-start(bf16[2,2,2,128,1024]{4,3,2,1,0:T(8,128)(2,1)} %copy-done.27) | copy-start | bytes 6291460
  305.2 26.3 %copy-start.53 = (bf16[2048,1024]{1,0:T(8,128)(2,1)S(1)}, bf16[2048,1024]{1,0:T(8,128)(2,1)}, u32[]{:S(2)}) copy-start(bf16[2048,1024]{1,0:T(8,128)(2,1)} %get-tuple-element.77) | copy-start | bytes 12582916
  307.0 121.0 %collective-permute-start.20 = (bf16[2,256,1024]{2,1,0:T(8,128)(2,1)}, bf16[2,256,1024]{2,1,0:T(8,128)(2,1)}, u32[]{:S(2)}, u32[]{:S(2)}) collective-permute-start(bf16[2,256,1024]{2,1,0:T(8,128)(2,1)} %get-tuple-element.34), channel_id=1, source_target_pairs={{0,3},{1,0},{2,1},{3,2},{4,7},{5,4},{6,5},{7,6},{8,11},{9,8},{10,9... | collective-permute-start | bytes 3145736 | tf_op jit(solution)/shard_map/ppermute | solution.py:23
  331.0 99.4 %collective-permute-start.19 = (bf16[2,256,1024]{2,1,0:T(8,128)(2,1)}, bf16[2,256,1024]{2,1,0:T(8,128)(2,1)}, u32[]{:S(2)}, u32[]{:S(2)}) collective-permute-start(bf16[2,256,1024]{2,1,0:T(8,128)(2,1)} %get-tuple-element.33), channel_id=1, source_target_pairs={{0,2},{1,3},{2,0},{3,1},{4,6},{5,7},{6,4},{7,5},{8,10},{9,11},{10,... | collective-permute-start | bytes 3145736 | tf_op jit(solution)/shard_map/ppermute | solution.py:23
  331.2 99.2 %collective-permute-start.18 = (bf16[2,256,1024]{2,1,0:T(8,128)(2,1)}, bf16[2,256,1024]{2,1,0:T(8,128)(2,1)}, u32[]{:S(2)}, u32[]{:S(2)}) collective-permute-start(bf16[2,256,1024]{2,1,0:T(8,128)(2,1)} %get-tuple-element.32), channel_id=1, source_target_pairs={{0,1},{1,2},{2,3},{3,0},{4,5},{5,6},{6,7},{7,4},{8,9},{9,10},{10,1... | collective-permute-start | bytes 3145736 | tf_op jit(solution)/shard_map/ppermute | solution.py:23
  353.7 29.3 %collective-permute-start.32 = (bf16[2,2,128,256]{3,2,1,0:T(8,128)(2,1)}, bf16[2,2,128,256]{3,2,1,0:T(8,128)(2,1)}, u32[]{:S(2)}, u32[]{:S(2)}) collective-permute-start(bf16[2,2,128,256]{3,2,1,0:T(8,128)(2,1)} %fusion.48), channel_id=1, source_target_pairs={{0,4},{4,0},{8,12},{12,8},{16,20},{20,16},{24,28},{28,24},{1,5},{5... | collective-permute-start | bytes 786440 | tf_op jit(solution)/shard_map/ppermute | solution.py:27
  356.0 28.4 %collective-permute-start.29 = (bf16[2,2,128,256]{3,2,1,0:T(8,128)(2,1)}, bf16[2,2,128,256]{3,2,1,0:T(8,128)(2,1)S(1)}, u32[]{:S(2)}, u32[]{:S(2)}) collective-permute-start(bf16[2,2,128,256]{3,2,1,0:T(8,128)(2,1)} %fusion.47), channel_id=1, source_target_pairs={{0,4},{4,0},{8,12},{12,8},{16,20},{20,16},{24,28},{28,24},{1,5},{5... | collective-permute-start | bytes 786440 | tf_op jit(solution)/shard_map/ppermute | solution.py:27
  374.5 8.6 %copy-start.42 = (f32[2,2,2,128,256]{4,3,2,1,0:T(8,128)S(1)}, f32[2,2,2,128,256]{4,3,2,1,0:T(8,128)}, u32[]{:S(2)}) copy-start(f32[2,2,2,128,256]{4,3,2,1,0:T(8,128)} %copy-done.41) | copy-start | bytes 3145732
  382.2 9.2 %copy-start.36 = (f32[2,2,2,128,256]{4,3,2,1,0:T(8,128)S(1)}, f32[2,2,2,128,256]{4,3,2,1,0:T(8,128)}, u32[]{:S(2)}) copy-start(f32[2,2,2,128,256]{4,3,2,1,0:T(8,128)} %copy-done.35) | copy-start | bytes 3145732
  382.9 1.9 collective-permute-start.26
  384.4 5.4 collective-permute-start.35
  384.7 46.2 %copy-start.3 = (bf16[2,256,1024]{2,1,0:T(8,128)(2,1)S(1)}, bf16[2,256,1024]{2,1,0:T(8,128)(2,1)}, u32[]{:S(2)}) copy-start(bf16[2,256,1024]{2,1,0:T(8,128)(2,1)} %param.15) | copy-start | bytes 3145732
  384.7 46.2 %copy-start.48 = (f32[2,256]{1,0:T(2,128)S(1)}, f32[2,256]{1,0:T(2,128)}, u32[]{:S(2)}) copy-start(f32[2,256]{1,0:T(2,128)} %copy-done.47) | copy-start | bytes 6148
  384.7 46.2 %copy-start.49 = (f32[2,256]{1,0:T(2,128)S(1)}, f32[2,256]{1,0:T(2,128)}, u32[]{:S(2)}) copy-start(f32[2,256]{1,0:T(2,128)} %add_rsqrt_fusion.1) | copy-start | bytes 6148
  384.8 64.9 %collective-permute-start.17 = (bf16[2,256,1024]{2,1,0:T(8,128)(2,1)S(1)}, bf16[2,256,1024]{2,1,0:T(8,128)(2,1)S(1)}, u32[]{:S(2)}, u32[]{:S(2)}) collective-permute-start(bf16[2,256,1024]{2,1,0:T(8,128)(2,1)S(1)} %copy-done.31), channel_id=1, source_target_pairs={{0,3},{1,0},{2,1},{3,2},{4,7},{5,4},{6,5},{7,6},{8,11},{9,8},{10,9... | collective-permute-start | bytes 3145736 | tf_op jit(solution)/shard_map/ppermute | solution.py:23
  389.8 5.3 collective-permute-start.33
  395.1 5.0 collective-permute-start.30
  400.1 5.0 collective-permute-start.27
  405.1 5.6 %collective-permute-start.36 = (bf16[2,128,256]{2,1,0:T(8,128)(2,1)S(1)}, bf16[2,128,256]{2,1,0:T(8,128)(2,1)S(1)}, u32[]{:S(2)}, u32[]{:S(2)}) collective-permute-start(bf16[2,128,256]{2,1,0:T(8,128)(2,1)S(1)} %fusion.52), channel_id=1, source_target_pairs={{0,8},{4,12},{8,0},{12,4},{16,24},{20,28},{24,16},{28,20},{1,9},{5... | collective-permute-start | bytes 393224 | tf_op jit(solution)/shard_map/ppermute | solution.py:27
  410.7 4.3 collective-permute-start.34
  414.9 4.3 collective-permute-start.31
  419.2 4.3 collective-permute-start.28
  423.5 4.3 collective-permute-start.37
  427.7 84.1 %collective-permute-start.16 = (bf16[2,256,1024]{2,1,0:T(8,128)(2,1)S(1)}, bf16[2,256,1024]{2,1,0:T(8,128)(2,1)S(1)}, u32[]{:S(2)}, u32[]{:S(2)}) collective-permute-start(bf16[2,256,1024]{2,1,0:T(8,128)(2,1)S(1)} %get-tuple-element.36), channel_id=1, source_target_pairs={{0,2},{1,3},{2,0},{3,1},{4,6},{5,7},{6,4},{7,5},{8,10},{9,11},{10,... | collective-permute-start | bytes 3145736 | tf_op jit(solution)/shard_map/ppermute | solution.py:23
  428.0 83.8 %collective-permute-start.15 = (bf16[2,256,1024]{2,1,0:T(8,128)(2,1)S(1)}, bf16[2,256,1024]{2,1,0:T(8,128)(2,1)S(1)}, u32[]{:S(2)}, u32[]{:S(2)}) collective-permute-start(bf16[2,256,1024]{2,1,0:T(8,128)(2,1)S(1)} %get-tuple-element.35), channel_id=1, source_target_pairs={{0,1},{1,2},{2,3},{3,0},{4,5},{5,6},{6,7},{7,4},{8,9},{9,10},{10,1... | collective-permute-start | bytes 3145736 | tf_op jit(solution)/shard_map/ppermute | solution.py:23
  430.3 81.5 %copy-start.22 = (bf16[2,256,1024]{2,1,0:T(8,128)(2,1)S(1)}, bf16[2,256,1024]{2,1,0:T(8,128)(2,1)}, u32[]{:S(2)}) copy-start(bf16[2,256,1024]{2,1,0:T(8,128)(2,1)} %param.29) | copy-start | bytes 3145732
  430.3 81.5 %copy-start.50 = (f32[1024]{0:T(1024)S(1)}, f32[1024]{0:T(1024)}, u32[]{:S(2)}) copy-start(f32[1024]{0:T(1024)} %convert_element_type.344) | copy-start | bytes 12292
  430.3 81.5 %copy-start.51 = (f32[1024]{0:T(1024)S(1)}, f32[1024]{0:T(1024)}, u32[]{:S(2)}) copy-start(f32[1024]{0:T(1024)} %convert_element_type.343) | copy-start | bytes 12292
  430.3 92.1 %collective-permute-start.38 = (bf16[2,2,128,1024]{3,2,1,0:T(8,128)(2,1)S(1)}, bf16[2,2,128,1024]{3,2,1,0:T(8,128)(2,1)S(1)}, u32[]{:S(2)}, u32[]{:S(2)}) collective-permute-start(bf16[2,2,128,1024]{3,2,1,0:T(8,128)(2,1)S(1)} %fusion.33), channel_id=1, source_target_pairs={{0,4},{4,0},{8,12},{12,8},{16,20},{20,16},{24,28},{28,24},{1,5},{5... | collective-permute-start | bytes 3145736 | tf_op jit(solution)/shard_map/ppermute | solution.py:27
  430.4 98.3 %collective-permute-start.41 = (bf16[2,2,128,1024]{3,2,1,0:T(8,128)(2,1)S(1)}, bf16[2,2,128,1024]{3,2,1,0:T(8,128)(2,1)S(1)}, u32[]{:S(2)}, u32[]{:S(2)}) collective-permute-start(bf16[2,2,128,1024]{3,2,1,0:T(8,128)(2,1)S(1)} %fusion.34), channel_id=1, source_target_pairs={{0,4},{4,0},{8,12},{12,8},{16,20},{20,16},{24,28},{28,24},{1,5},{5... | collective-permute-start | bytes 3145736 | tf_op jit(solution)/shard_map/ppermute | solution.py:27
  515.9 4.1 collective-permute-start.21
  520.1 5.4 collective-permute-start.22
  525.4 1.7 collective-permute-start.23
  525.6 16.1 %collective-permute-start.39 = (bf16[2,128,1024]{2,1,0:T(8,128)(2,1)S(1)}, bf16[2,128,1024]{2,1,0:T(8,128)(2,1)S(1)}, u32[]{:S(2)}, u32[]{:S(2)}) collective-permute-start(bf16[2,128,1024]{2,1,0:T(8,128)(2,1)S(1)} %fusion.41), channel_id=1, source_target_pairs={{0,16},{4,20},{8,24},{12,28},{16,0},{20,4},{24,8},{28,12},{1,17},{... | collective-permute-start | bytes 1572872 | tf_op jit(solution)/shard_map/ppermute | solution.py:27
  527.2 4.2 collective-permute-start.24
  531.4 9.7 %collective-permute-start.25 = (f32[96,128]{1,0:T(8,128)S(1)}, f32[96,128]{1,0:T(8,128)S(1)}, u32[]{:S(2)}, u32[]{:S(2)}) collective-permute-start(f32[96,128]{1,0:T(8,128)S(1)} %add.417), channel_id=1, source_target_pairs={{0,16},{4,20},{8,24},{12,28},{16,0},{20,4},{24,8},{28,12},{1,17},{... | collective-permute-start | bytes 147464 | tf_op jit(solution)/shard_map/ppermute | solution.py:27
  532.5 14.0 %collective-permute-start.42 = (bf16[2,128,1024]{2,1,0:T(8,128)(2,1)S(1)}, bf16[2,128,1024]{2,1,0:T(8,128)(2,1)S(1)}, u32[]{:S(2)}, u32[]{:S(2)}) collective-permute-start(bf16[2,128,1024]{2,1,0:T(8,128)(2,1)S(1)} %fusion.42), channel_id=1, source_target_pairs={{0,8},{4,12},{8,0},{12,4},{16,24},{20,28},{24,16},{28,20},{1,9},{5... | collective-permute-start | bytes 1572872 | tf_op jit(solution)/shard_map/ppermute | solution.py:27
  541.9 9.2 %collective-permute-start.40 = (bf16[128,1024]{1,0:T(8,128)(2,1)S(1)}, bf16[128,1024]{1,0:T(8,128)(2,1)S(1)}, u32[]{:S(2)}, u32[]{:S(2)}) collective-permute-start(bf16[128,1024]{1,0:T(8,128)(2,1)S(1)} %fusion.45), channel_id=1, source_target_pairs={{0,8},{4,12},{8,0},{12,4},{16,24},{20,28},{24,16},{28,20},{1,9},{5... | collective-permute-start | bytes 786440 | tf_op jit(solution)/shard_map/ppermute | solution.py:27
  546.7 6.4 %collective-permute-start.43 = (bf16[128,1024]{1,0:T(8,128)(2,1)S(1)}, bf16[128,1024]{1,0:T(8,128)(2,1)S(1)}, u32[]{:S(2)}, u32[]{:S(2)}) collective-permute-start(bf16[128,1024]{1,0:T(8,128)(2,1)S(1)} %fusion.46), channel_id=1, source_target_pairs={{0,16},{4,20},{8,24},{12,28},{16,0},{20,4},{24,8},{28,12},{1,17},{... | collective-permute-start | bytes 786440 | tf_op jit(solution)/shard_map/ppermute | solution.py:27
  (35 other events, 153.0 us)

commit v2 on v1

--- a/solution.py
+++ b/solution.py
@@ -19,8 +19,8 @@
 BF16 = jnp.bfloat16
 
 
-def shifted(array, axis_name, size, shift):
-    return lax.ppermute(array, axis_name, [(i, (i + shift) % size) for i in range(size)])
+def moved(array, axis_name, pairs):
+    return lax.ppermute(array, axis_name, pairs)
 
 
 def swapped(array, axis_name, size, bit):
@@ -28,23 +28,36 @@
 
 
 def gather_tokens(block, axis_name, size, me):
+    from_left, from_right = [block], [block]
+    for k in range(1, size):
+        right = [(i, i + 1) for i in range(k - 1, size - 1)]
+        left = [(i + 1, i) for i in range(size - k)]
+        from_left.append(moved(from_left[-1], axis_name, right))
+        from_right.append(moved(from_right[-1], axis_name, left))
     whole = jnp.zeros((block.shape[0], size) + block.shape[1:], block.dtype)
-    pieces = [block] + [shifted(block, axis_name, size, k) for k in range(1, size)]
-    for k, piece in enumerate(pieces):
+    for k in range(size):
+        piece = block if k == 0 else jnp.where(me >= k, from_left[k], from_right[size - k])
         owner = lax.rem(me - k + size, size)
         whole = lax.dynamic_update_slice_in_dim(whole, piece[:, None], owner, 1)
     return whole
 
 
-def scatter_tokens(parts, axis_name, size, me):
+def scatter_tokens(parts, axis_name, size, me, between=None):
     def part_for(owner):
-        return lax.dynamic_index_in_dim(parts, owner, 1, keepdims=False)
-
-    total = part_for(me).astype(F32)
-    for k in range(1, size):
-        sent = part_for(lax.rem(me + k, size)).astype(BF16)
-        total = total + shifted(sent, axis_name, size, k).astype(F32)
-    return total
+        return lax.dynamic_index_in_dim(parts, jnp.clip(owner, 0, size - 1), 1, keepdims=False).astype(F32)
+
+    from_left = from_right = None
+    for step in range(1, size):
+        to_right, to_left = part_for(size - step + me), part_for(step - size + me)
+        if step > 1:
+            to_right, to_left = to_right + from_left.astype(F32), to_left + from_right.astype(F32)
+        right = [(i, i + 1) for i in range(step)]
+        left = [(size - 1 - i, size - 2 - i) for i in range(step)]
+        from_left = moved(to_right.astype(BF16), axis_name, right)
+        from_right = moved(to_left.astype(BF16), axis_name, left)
+        if between is not None:
+            from_left, from_right = between(step, from_left, from_right)
+    return part_for(me) + from_left.astype(F32) + from_right.astype(F32)
 
 
 def bits_of(size):
@@ -77,15 +90,13 @@
     return held
 
 
-def sum_everywhere(vector, axes):
-    for axis_name, size in axes:
-        for bit in bits_of(size):
-            vector = vector + swapped(vector, axis_name, size, bit)
-    return vector
+def sum_stages(axes):
+    return [(axis_name, size, bit) for axis_name, size in axes for bit in bits_of(size)]
 
 
 def attention_kernel(
-    projected_ref, grad_ref, cos_ref, sin_ref, start_ref, out_ref, grads_ref,
+    query_ref, key_ref, value_ref, grad_ref, cos_ref, sin_ref, start_ref,
+    out_ref, grad_query_ref, grad_key_ref, grad_value_ref,
     queries_t, outputs_t, keys_sum, values_sum,
 ):
     length = cos_ref.shape[1]
@@ -104,12 +115,12 @@
     def rot_back(u):
         return u * cosine - partner(u) * sine
 
-    queries = (rot(projected_ref[0, 0]) * scale).astype(BF16)
-    rotated = rot(projected_ref[1, 0])
+    queries = (rot(query_ref[0]) * scale).astype(BF16)
+    rotated = rot(key_ref[0])
     keys = rotated.astype(BF16)
     keys_t = rotated.T.astype(BF16)
-    values = projected_ref[2, 0].astype(BF16)
-    values_t = projected_ref[2, 0].T.astype(BF16)
+    values = value_ref[0].astype(BF16)
+    values_t = value_ref[0].T.astype(BF16)
     grads = grad_ref[0]
 
     keys_sum[...] = jnp.zeros_like(keys_sum)
@@ -142,33 +153,29 @@
             keys_sum[:seen, columns] += jnp.dot(grad_scores, query, preferred_element_type=F32)
             values_sum[:seen, columns] += jnp.dot(weights, grad, preferred_element_type=F32)
     out_ref[0] = outputs_t[...].T.astype(BF16)
-    grads_ref[0, 0] = (rot_back(queries_t[...].T) * scale).astype(BF16)
-    grads_ref[1, 0] = rot_back(keys_sum[...]).astype(BF16)
-    grads_ref[2, 0] = values_sum[...].astype(BF16)
+    grad_query_ref[0] = (rot_back(queries_t[...].T) * scale).astype(BF16)
+    grad_key_ref[0] = rot_back(keys_sum[...]).astype(BF16)
+    grad_value_ref[0] = values_sum[...].astype(BF16)
 
 
 def attention(projected, grad_attended, cosine, sine, starts):
-    _, count, length, width = projected.shape
+    count, length, width = grad_attended.shape
     pairs = width // PAIR
     work = count * length * length * width
     return pl.pallas_call(
         attention_kernel,
         grid=(count, pairs),
-        out_shape=(
-            jax.ShapeDtypeStruct((count, length, width), BF16),
-            jax.ShapeDtypeStruct((3, count, length, width), BF16),
-        ),
+        out_shape=(jax.ShapeDtypeStruct((count, length, width), BF16),) * 4,
         in_specs=[
-            pl.BlockSpec((3, 1, length, PAIR), lambda s, h: (0, s, 0, h)),
+            pl.BlockSpec((1, length, PAIR), lambda s, h: (s, 0, h)),
+            pl.BlockSpec((1, length, PAIR), lambda s, h: (s, 0, h + pairs)),
+            pl.BlockSpec((1, length, PAIR), lambda s, h: (s, 0, h + 2 * pairs)),
             pl.BlockSpec((1, length, PAIR), lambda s, h: (s, 0, h)),
             pl.BlockSpec((1, length, PAIR), lambda s, h: (s, 0, 0)),
             pl.BlockSpec((1, length, PAIR), lambda s, h: (s, 0, 0)),
             pl.BlockSpec((1, 1, length), lambda s, h: (s, 0, 0)),
         ],
-        out_specs=(
-            pl.BlockSpec((1, length, PAIR), lambda s, h: (s, 0, h)),
-            pl.BlockSpec((3, 1, length, PAIR), lambda s, h: (0, s, 0, h)),
-        ),
+        out_specs=(pl.BlockSpec((1, length, PAIR), lambda s, h: (s, 0, h)),) * 4,
         scratch_shapes=[
             pltpu.VMEM((PAIR, length), F32),
             pltpu.VMEM((PAIR, length), F32),
@@ -181,7 +188,7 @@
             transcendentals=work // (2 * HEAD_DIM),
         ),
         name="attention",
-    )(projected, grad_attended, cosine, sine, starts)
+    )(projected, projected, projected, grad_attended, cosine, sine, starts)
 
 
 def make_shards(dp_size, tensor_size):
@@ -202,17 +209,17 @@
         def gather(block):
             return gather_tokens(block, "tensor", tensor_size, tensor_index).reshape(rows, width)
 
-        def scatter(parts):
+        def scatter(parts, between=None):
             parts = parts.reshape(count, tensor_size, own_length, width)
-            return scatter_tokens(parts, "tensor", tensor_size, tensor_index)
+            return scatter_tokens(parts, "tensor", tensor_size, tensor_index, between)
 
         hidden_rows = gather(hidden_in)
-        attn_w = jnp.concatenate([w_qkv, w_out[None]], 0)
-        attn_full = gather_rows(attn_w, "dp", dp_size, dp_index, order_a)
-        full_qkv = attn_full[:, :3].transpose(1, 0, 2, 3).reshape(3, width, local)
-        full_out = attn_full[:, 3].reshape(width, local)
+        attn_w = jnp.concatenate([w_qkv[0], w_qkv[1], w_qkv[2], w_out], 1)
+        attn_full = gather_rows(attn_w, "dp", dp_size, dp_index, order_a).reshape(width, 4 * local)
+        full_qkv, full_out = attn_full[:, : 3 * local], attn_full[:, 3 * local :]
         full_up = gather_rows(w_up, "dp", dp_size, dp_index, order_b).reshape(width, local_units)
-        cot_rows = gather(cotangent)
+        hidden_rows, later_cot = lax.optimization_barrier((hidden_rows, cotangent))
+        cot_rows = gather(later_cot)
         full_down = gather_rows(w_down, "dp", dp_size, dp_index, order_a).reshape(width, local_units)
 
         zeros = jnp.sum((segments == 0).astype(jnp.int32), -1, keepdims=True)
@@ -237,18 +244,15 @@
         bias_qkv = lax.dynamic_slice_in_dim(b_qkv, tensor_index * local, local, 1)
         bias_up = lax.dynamic_slice_in_dim(b_up, tensor_index * local_units, local_units, 0)
 
-        projected = (
-            jnp.einsum("rd,cde->cre", first, full_qkv, preferred_element_type=F32)
-            + bias_qkv[:, None, :]
-        )
+        projected = jnp.dot(first, full_qkv, preferred_element_type=F32) + bias_qkv.reshape(-1)
         grad_attended = jnp.dot(cot_rows, full_out, preferred_element_type=F32).astype(BF16)
-        attended, grad_projected = attention(
-            projected.reshape(3, count, length, local),
+        attended, *grad_parts = attention(
+            projected.reshape(count, length, 3 * local),
             grad_attended.reshape(count, length, local),
             cosine, sine, starts[:, None, :],
         )
         attended = attended.reshape(rows, local)
-        grad_projected = grad_projected.reshape(3, rows, local)
+        grad_projected = jnp.concatenate(grad_parts, -1).reshape(rows, 3 * local)
 
         units = jnp.dot(second, full_up, preferred_element_type=F32) + bias_up
         cumulative = 0.5 * (1.0 + lax.erf(units * (1.0 / math.sqrt(2.0))))
@@ -262,13 +266,47 @@
         hidden = hidden_in.astype(F32)
         block_out = (hidden + scatter(branch) + b_out + b_down).astype(BF16)
 
-        grad_first = jnp.einsum("cre,cde->rd", grad_projected, full_qkv, preferred_element_type=F32)
+        grad_first = lax.dot_general(grad_projected, full_qkv, BY_COLUMNS, preferred_element_type=F32)
         grad_second = lax.dot_general(grad_units, full_up, BY_COLUMNS, preferred_element_type=F32)
         norm_terms = [
             jnp.sum(grad_first * normed, 0), jnp.sum(grad_first, 0),
             jnp.sum(grad_second * normed, 0), jnp.sum(grad_second, 0),
         ]
-        e = scatter(grad_first * ln1_gain + grad_second * ln2_gain)
+        def to_owners(part, order):
+            split = part.reshape((dp_size, part.shape[0] // dp_size) + part.shape[1:])
+            return scatter_rows(split, "dp", dp_size, dp_index, bits[:1] + order)
+
+        xy, yx = bits[1:], bits[:0:-1]
+        grad_w_down = to_owners(lax.dot_general(cot_rows, activated, BY_ROWS, preferred_element_type=F32), xy)
+        grad_w_up = to_owners(lax.dot_general(second, grad_units, BY_ROWS, preferred_element_type=F32), yx)
+        attn_parts = jnp.concatenate([
+            lax.dot_general(first, grad_projected, BY_ROWS, preferred_element_type=F32),
+            lax.dot_general(cot_rows, attended, BY_ROWS, preferred_element_type=F32),
+        ], 1)
+        grad_attn = to_owners(attn_parts, yx)
+        grad_w_out = grad_attn[:, 3 * local :]
+        grad_w_qkv = jnp.stack([grad_attn[:, c * local : (c + 1) * local] for c in range(3)])
+
+        padded_qkv = lax.dynamic_update_slice_in_dim(
+            jnp.zeros((3, width), F32),
+            jnp.sum(grad_projected, 0, dtype=F32).reshape(3, local), tensor_index * local, 1,
+        )
+        padded_up = lax.dynamic_update_slice_in_dim(
+            jnp.zeros(b_up.shape, F32), jnp.sum(grad_units, 0, dtype=F32), tensor_index * local_units, 0
+        )
+        cot_sums = jnp.sum(cotangent, (0, 1), dtype=F32)
+        vector = jnp.concatenate(norm_terms + [padded_qkv.reshape(-1), cot_sums, padded_up])
+        vector = [vector.reshape(-1, 128)]
+        stages = sum_stages((("tensor", tensor_size), ("dp", dp_size)))
+        share = -(-len(stages) // (tensor_size - 1))
+
+        def sum_some(step, left, right):
+            for stage in stages[(step - 1) * share : step * share]:
+                vector[0] = vector[0] + swapped(vector[0], *stage)
+            left, right, vector[0] = lax.optimization_barrier((left, right, vector[0]))
+            return left, right
+
+        e = scatter(grad_first * ln1_gain + grad_second * ln2_gain, sum_some)
         own_normed, own_scaling = layer_normed(hidden)
         grad_in = cotangent.astype(F32) + own_scaling * (
             e
@@ -276,29 +314,7 @@
             - own_normed * jnp.mean(e * own_normed, -1, keepdims=True)
         )
 
-        def to_owners(part, order):
-            split = part.reshape((dp_size, part.shape[0] // dp_size) + part.shape[1:])
-            return scatter_rows(split, "dp", dp_size, dp_index, bits[:1] + order)
-
-        xy, yx = bits[1:], bits[:0:-1]
-        grad_w_down = to_owners(lax.dot_general(cot_rows, activated, BY_ROWS, preferred_element_type=F32), xy)
-        grad_w_out = to_owners(lax.dot_general(cot_rows, attended, BY_ROWS, preferred_element_type=F32), xy)
-        grad_w_up = to_owners(lax.dot_general(second, grad_units, BY_ROWS, preferred_element_type=F32), yx)
-        grad_w_qkv = jnp.stack([
-            to_owners(lax.dot_general(first, grad_projected[c], BY_ROWS, preferred_element_type=F32), yx if c else xy)
-            for c in range(3)
-        ])
-
-        padded_qkv = lax.dynamic_update_slice_in_dim(
-            jnp.zeros((3, width), F32), jnp.sum(grad_projected, 1, dtype=F32), tensor_index * local, 1
-        )
-        padded_up = lax.dynamic_update_slice_in_dim(
-            jnp.zeros(b_up.shape, F32), jnp.sum(grad_units, 0, dtype=F32), tensor_index * local_units, 0
-        )
-        cot_sums = jnp.sum(cotangent, (0, 1), dtype=F32)
-        vector = jnp.concatenate(norm_terms + [padded_qkv.reshape(-1), cot_sums, padded_up])
-        vector = vector.reshape(-1, 128)
-        vector = sum_everywhere(vector, (("tensor", tensor_size), ("dp", dp_size))).reshape(-1)
+        vector = vector[0].reshape(-1)
         g1, b1, g2, b2, qkv, cot_sum, up = jnp.split(
             vector, [width, 2 * width, 3 * width, 4 * width, 7 * width, 8 * width]
         )

time: 562 us -> 509 us (0.906)
  waiting for transfers between devices: 239 us -> 191 us
  other arithmetic: 51.6 us -> 61.7 us
  starting transfers between devices: 72.1 us -> 63.6 us
  local copies, waits for them, and re-layouts: 63.8 us -> 57 us
    ppermute x32 -> x23, waiting for transfers between devices: 65.6 us -> 21 us  [swapped(): return lax.ppermute(array, axis_name, [(i, i ^ bit) for i in range(size)])]
    dynamic_slice x0 -> x3, local copies, waits for them, and re-layouts: none -> 16.9 us  [the longest x2 11.5 us: scatter_rows(): keep = lax.dynamic_index_in_dim(held, mine, at, keepdims=False)]
    ppermute x32 -> x23, starting transfers between devices: 29.8 us -> 15.9 us  [swapped(): return lax.ppermute(array, axis_name, [(i, i ^ bit) for i in range(size)])]
    dot_general x2 -> x0, local copies, waits for them, and re-layouts: 13.2 us -> none  [the longest x1 6.7 us: shards(): lax.dot_general(first, grad_projected[c], BY_ROWS, preferred_element_type...]
    convert_element_type x1 -> x7, other arithmetic: 0.68 us -> 10.9 us  [the longest x3 5.16 us: scatter_tokens(): from_right = moved(to_left.astype(BF16), axis_name, left)]
    dynamic_update_slice x0 -> x6, other arithmetic: none -> 7.99 us  [gather_tokens(): whole = lax.dynamic_update_slice_in_dim(whole, piece[:, None], owner, 1)]
    convert_element_type x3 -> x2, other arithmetic: 7.61 us -> 0.01 us  [shards(): first = (normed * ln1_gain + ln1_bias).astype(BF16)]
    dot_general x1, matrix products: 1.32 us -> 8.49 us  [shards(): lax.dot_general(attended, full_out, BY_COLUMNS, preferred_element_type=F32)]
  transfers between devices with their start and end apart: 44 -> 47, of which waited for: 23 -> 18; matrix products, arithmetic and copies ran while one was open for 27% -> 30% of each run, Pallas kernels for 8% -> 9%
where the time goes in v2:
time: 509 us; the launch traced here: 500 us
  waiting for transfers between devices  191 us (38%)
  matrix products  79.2 us (16%)
  starting transfers between devices  63.6 us (12%)
  other arithmetic  61.7 us (12%)
  local copies, waits for them, and re-layouts  57 us (11%)
  Pallas kernels  45.4 us (9%)
    ppermute x24, waiting for transfers between devices, moved(): return lax.ppermute(array, axis_name, pairs)  170 us
    ppermute x24, starting transfers between devices, moved(): return lax.ppermute(array, axis_name, pairs)  47.8 us
    pallas_call x1, Pallas kernels, attention(): pl.pallas_call(attention_kernel, grid=(count, pairs), out_shape=(jax.Shap...  45.4 us
    ppermute x23, waiting for transfers between devices, swapped(): return lax.ppermute(array, axis_name, [(i, i ^ bit) for i in range(size)])  21 us
    ppermute x23, starting transfers between devices, swapped(): return lax.ppermute(array, axis_name, [(i, i ^ bit) for i in range(size)])  15.9 us
    dynamic_slice x2, local copies, waits for them, and re-layouts, scatter_rows(): keep = lax.dynamic_index_in_dim(held, mine, at, keepdims=False)  11.5 us
    another operation x16, other arithmetic, gather_rows(): jnp.stack([jnp.where(upper, other, held), jnp.where(upper, held, other)])  11.5 us
    dot_general x1, matrix products, shards(): jnp.dot(cot_rows, full_down, preferred_element_type=F32) * slope  10.5 us
  transfers between devices with their start and end apart: 47, of which 18 were waited for; matrix products, arithmetic and copies ran while one was open for 30% of the time, Pallas kernels for 9%

profile of v2, /device:TPU:0, one launch (start us, length us, event | category | flops | bytes accessed | tf_op | source)
XLA Modules:
  0.0 500.1 jit_solution(2710364211478502787)
XLA Ops:
  1.9 6.6 %collective-permute-start = (bf16[2,256,1024]{2,1,0:T(8,128)(2,1)}, bf16[2,256,1024]{2,1,0:T(8,128)(2,1)}, u32[]{:S(2)}, u32[]{:S(2)}) collective-permute-start(bf16[2,256,1024]{2,1,0:T(8,128)(2,1)} %param.15), channel_id=1, source_target_pairs={{0,1},{1,2},{2,3},{4,5},{5,6},{6,7},{8,9},{9,10},{10,11},{12,13},{... | collective-permute-start | bytes 3145736 | tf_op jit(solution)/shard_map/ppermute | solution.py:23
  8.5 2.0 collective-permute-start.15
  14.4 1.5 convert_reduce_fusion.3
  16.8 1.6 fusion.28
  19.8 5.6 %fusion.48 = (f32[2,1024,128]{2,1,0:T(8,128)}, f32[2,1024,128]{2,1,0:T(8,128)}) fusion(f32[128]{0:T(128)S(1)} %fusion.71, f32[2,1024]{1,0:T(2,128)S(1)} %get-tuple-element.53, pred[128]{0:T(512)(128)(4,1)S(1)} %get-tuple-element.106, pred[128]{0:T(512)(128)(4,1)S(1)} %get-tuple-element.107), kind=kLoop, calls=%fused_computation.89 | loop fusion | flops 1310720 | bytes 2106112 | tf_op jit(solution)/shard_map/jit(_where)/select_n | solution.py:234
  26.3 1.6 collective-permute-start.16
  32.7 5.8 %collective-permute-done.16 = bf16[2,128,1024]{2,1,0:T(8,128)(2,1)S(1)} collective-permute-done((bf16[2,128,1024]{2,1,0:T(8,128)(2,1)S(1)}, bf16[2,128,1024]{2,1,0:T(8,128)(2,1)S(1)}, u32[]{:S(2)}, u32[]{:S(2)}) %collective-permute-start.16) | collective-permute-done | bytes 524320 | tf_op jit(solution)/shard_map/ppermute | solution.py:27
  40.6 3.3 collective-permute-done.19
  49.5 2.8 collective-permute-done.7
  56.5 13.2 %collective-permute-done.2 = bf16[2,256,1024]{2,1,0:T(8,128)(2,1)} collective-permute-done((bf16[2,256,1024]{2,1,0:T(8,128)(2,1)}, bf16[2,256,1024]{2,1,0:T(8,128)(2,1)}, u32[]{:S(2)}, u32[]{:S(2)}) %collective-permute-start.2) | collective-permute-done | bytes 1048608 | tf_op jit(solution)/shard_map/ppermute | solution.py:23
  71.4 2.1 select_bitcast_fusion.1
  75.1 18.0 %collective-permute-done.3 = bf16[2,256,1024]{2,1,0:T(8,128)(2,1)S(1)} collective-permute-done((bf16[2,256,1024]{2,1,0:T(8,128)(2,1)}, bf16[2,256,1024]{2,1,0:T(8,128)(2,1)S(1)}, u32[]{:S(2)}, u32[]{:S(2)}) %collective-permute-start.3) | collective-permute-done | bytes 1048608 | tf_op jit(solution)/shard_map/ppermute | solution.py:23
  93.5 1.7 bitcast_dynamic-update-slice_fusion.5
  95.2 1.7 bitcast_dynamic-update-slice_fusion.4
  98.2 4.6 collective-permute-start.9
  104.9 8.7 %multiply_convert_fusion = (bf16[2048,1024]{1,0:T(8,128)(2,1)S(1)}, f32[2048,1024]{1,0:T(8,128)}) fusion(f32[1024]{0:T(1024)S(1)} %dynamic-slice_convert_fusion.7, bf16[1024,1024]{1,0:T(8,128)(2,1)S(1)} %bitcast.281, bf16[2048,1024]{1,0:T(8,128)(2,1)S(1)} %bitcast.261, f32[1024]{0:T(1024)S(1)} %convert_element_type.265, ...), kind=kOutput, calls=%fused_computation.24 | convolution fusion | flops 4320133120 | bytes 18903040 | tf_op jit(solution)/shard_map/dot_general | solution.py:257
  113.6 5.6 %collective-permute-done.10 = bf16[2,256,1024]{2,1,0:T(8,128)(2,1)S(1)} collective-permute-done((bf16[2,256,1024]{2,1,0:T(8,128)(2,1)S(1)}, bf16[2,256,1024]{2,1,0:T(8,128)(2,1)S(1)}, u32[]{:S(2)}, u32[]{:S(2)}) %collective-permute-start.10) | collective-permute-done | bytes 1048608 | tf_op jit(solution)/shard_map/ppermute | solution.py:23
  121.5 6.0 %convolution_add_fusion.1 = f32[2048,768]{1,0:T(8,128)} fusion(f32[768]{0:T(1024)S(1)} %reshape.173, bf16[1024,1024]{1,0:T(8,128)(2,1)S(1)} %bitcast.275, bf16[2048,1024]{1,0:T(8,128)(2,1)S(1)} %bitcast.262, f32[1024]{0:T(1024)S(1)} %convert_element_type.255, f32[1024]{0:T(1024)S(1)} %convert_element_type.254, f32[2048]{0:T(1024)S(1)} %add_rsqrt_fusion, ...), kind=kOutput, calls=%fused_computation.31 | convolution fusion | flops 3235381248 | bytes 12087296 | tf_op jit(solution)/shard_map/dot_general | solution.py:247
  127.5 31.2 %collective-permute-done.11 = bf16[2,256,1024]{2,1,0:T(8,128)(2,1)S(1)} collective-permute-done((bf16[2,256,1024]{2,1,0:T(8,128)(2,1)S(1)}, bf16[2,256,1024]{2,1,0:T(8,128)(2,1)S(1)}, u32[]{:S(2)}, u32[]{:S(2)}) %collective-permute-start.11) | collective-permute-done | bytes 1048608 | tf_op jit(solution)/shard_map/ppermute | solution.py:23
  160.7 7.2 %fusion.86 = f32[2048,1024]{1,0:T(8,128)} fusion(bf16[2048,1024]{1,0:T(8,128)(2,1)S(1)} %get-tuple-element.104, bf16[1024,1024]{1,0:T(8,128)(2,1)S(1)} %bitcast.283), kind=kOutput, calls=%fused_computation.213 | convolution fusion | flops 4294967296 | bytes 14680064 | tf_op jit(solution)/shard_map/dot_general | solution.py:265
  167.9 2.5 broadcast.135
  171.5 11.9 %collective-permute-done.12 = bf16[2,256,1024]{2,1,0:T(8,128)(2,1)S(1)} collective-permute-done((bf16[2,256,1024]{2,1,0:T(8,128)(2,1)S(1)}, bf16[2,256,1024]{2,1,0:T(8,128)(2,1)S(1)}, u32[]{:S(2)}, u32[]{:S(2)}) %collective-permute-start.12) | collective-permute-done | bytes 1048608 | tf_op jit(solution)/shard_map/ppermute | solution.py:23
  187.6 6.5 %copy.63 = bf16[2048,1024]{0,1:T(8,128)(2,1)} copy(bf16[2048,1024]{1,0:T(8,128)(2,1)} %bitcast.30) | data formatting | bytes 8388608 | tf_op jit(solution)/shard_map/reshape | solution.py:210
  194.2 3.7 convolution_convert_fusion
  197.9 10.5 %convert_reduce_fusion.1 = (f32[1024]{0:T(1024)S(1)}, bf16[2048,1024]{1,0:T(8,128)(2,1)S(1)}) fusion(f32[2048,1024]{1,0:T(8,128)} %get-tuple-element.105, f32[1024]{0:T(1024)S(1)} %dynamic-slice_convert_fusion.7, bf16[2048,1024]{1,0:T(8,128)(2,1)} %bitcast.30, bf16[1024,1024]{1,0:T(8,128)(2,1)S(1)} %bitcast.284), kind=kOutput, calls=%fused_computation.22 | convolution fusion | flops 4322229248 | bytes 18882560 | tf_op jit(solution)/shard_map/dot_general | solution.py:262
  208.4 5.2 %fusion.73 = f32[1024,1024]{1,0:T(8,128)S(1)} fusion(bf16[2048,1024]{1,0:T(8,128)(2,1)S(1)} %get-tuple-element.103, bf16[2048,1024]{1,0:T(8,128)(2,1)S(1)} %bitcast.263, f32[1024]{0:T(1024)S(1)} %convert_element_type.265, f32[1024]{0:T(1024)S(1)} %convert_element_type.264, f32[2048]{0:T(1024)S(1)} %add_rsqrt_fusion, f32[2048]{0:T(1024)S(1)} %broadcast_multiply_fusion), kind=kOutput, calls=%fused_computation.206 | convolution fusion | flops 4307550208 | bytes 12607488 | tf_op jit(solution)/shard_map/dot_general | solution.py:281
  213.7 7.0 %fusion.87 = f32[2048,1024]{1,0:T(8,128)} fusion(bf16[2048,1024]{1,0:T(8,128)(2,1)S(1)} %get-tuple-element.103, bf16[1024,1024]{1,0:T(8,128)(2,1)S(1)} %bitcast.282), kind=kOutput, calls=%fused_computation.214 | convolution fusion | flops 4294967296 | bytes 14680064 | tf_op jit(solution)/shard_map/dot_general | solution.py:270
  221.7 4.5 fusion.19
  229.1 45.4 %attention.1 = (bf16[2,1024,256]{2,1,0:T(8,128)(2,1)S(1)}, bf16[2,1024,256]{2,1,0:T(8,128)(2,1)S(1)}, bf16[2,1024,256]{2,1,0:T(8,128)(2,1)S(1)}, bf16[2,1024,256]{2,1,0:T(8,128)(2,1)S(1)}) custom-call(f32[2,1024,768]{2,1,0:T(8,128)} %bitcast.287, f32[2,1024,768]{2,1,0:T(8,128)} %bitcast.288, f32[2,1024,768]{2,1,0:T(8,128)} %bitcast.289, ...), custom_call_target="tpu_custom_call" | custom-call | flops 16106127360 | bytes 12582912 | tf_op jit(solution)/shard_map/attention/pallas_call | solution.py:165
  275.3 4.0 fusion.77
  279.3 3.5 fusion.88
  282.8 2.5 pad_maximum_fusion
  285.3 6.6 %reshape_reshape.19 = f32[2,2,2,128,1024]{3,2,1,0,4:T(2,128)} reshape(f32[1024,1024]{0,1:T(8,128)} %pad_maximum_fusion) | data formatting | bytes 8388608 | tf_op jit(solution)/shard_map/reshape;reshape | solution.py:82
  291.9 5.4 %constant_dynamic-slice_fusion = bf16[2,2,1,128,1024]{3,2,1,0,4:T(2,128)(2,1)} fusion(f32[2,2,2,128,1024]{3,2,1,0,4:T(2,128)} %reshape_reshape.19, s32[]{:T(128)S(6)} %select_n.323), kind=kLoop, calls=%fused_computation.163 | loop fusion | bytes 2097156 | tf_op jit(solution)/shard_map/jit(dynamic_index_in_dim)/dynamic_slice | solution.py:87
  297.3 5.9 %copy.69 = bf16[2,2,1,128,1024]{4,3,1,0,2:T(8,128)(2,1)} copy(bf16[2,2,1,128,1024]{3,2,1,0,4:T(2,128)(2,1)} %constant_dynamic-slice_fusion) | data formatting | bytes 2097152
  303.5 8.5 %convolution_add_fusion = f32[2048,1024]{1,0:T(8,128)} fusion(f32[2048,1024]{1,0:T(8,128)} %fusion.86, bf16[2048,256]{1,0:T(8,128)(2,1)S(1)} %bitcast.250, bf16[1024,1024]{1,0:T(8,128)(2,1)} %bitcast.277), kind=kOutput, calls=%fused_computation.27 | convolution fusion | flops 1075838976 | bytes 18350080 | tf_op jit(solution)/shard_map/dot_general | solution.py:264
  312.0 10.3 %fusion.80 = (f32[1024]{0:T(1024)S(1)}, f32[1024]{0:T(1024)S(1)}, f32[2048,1024]{1,0:T(8,128)}, f32[1024]{0:T(1024)S(1)}, f32[1024]{0:T(1024)S(1)}) fusion(f32[2048,1024]{1,0:T(8,128)} %fusion.87, f32[2048]{0:T(1024)S(1)} %add_rsqrt_fusion, f32[2048]{0:T(1024)S(1)} %broadcast_multiply_fusion, bf16[2048,1024]{1,0:T(8,128)(2,1)S(1)} %bitcast.265, ...), kind=kOutput, calls=%fused_computation.209 | convolution fusion | flops 3246387200 | bytes 25731072 | tf_op jit(solution)/shard_map/dot_general | solution.py:269
  322.8 5.4 %constant_dynamic-slice_fusion.1 = f32[2,2,1,128,1024]{3,2,1,0,4:T(1,128)} fusion(f32[2,2,2,128,1024]{3,2,1,0,4:T(2,128)} %reshape_reshape.19, s32[]{:T(128)S(6)} %select_n.322), kind=kLoop, calls=%fused_computation.164 | loop fusion | bytes 4194308 | tf_op jit(solution)/shard_map/jit(dynamic_index_in_dim)/dynamic_slice | solution.py:86
  328.2 3.6 fusion.51
  331.8 2.4 collective-permute-start.30
  334.2 3.9 fusion.54
  338.0 6.1 %copy.60 = f32[2,2,1,128,1024]{4,3,1,0,2:T(8,128)} copy(f32[2,2,1,128,1024]{3,2,1,0,4:T(1,128)} %constant_dynamic-slice_fusion.1) | data formatting | bytes 4194304 | tf_op jit(solution)/shard_map/jit(dynamic_index_in_dim)/dynamic_slice | solution.py:86
  344.1 2.2 collective-permute-start.27
  348.5 2.0 bitcast_add_fusion.2
  351.3 1.6 bitcast_add_fusion
  353.1 17.0 %collective-permute-done.27 = bf16[2,256,1024]{2,1,0:T(8,128)(2,1)S(1)} collective-permute-done((bf16[2,256,1024]{2,1,0:T(8,128)(2,1)}, bf16[2,256,1024]{2,1,0:T(8,128)(2,1)S(1)}, u32[]{:S(2)}, u32[]{:S(2)}) %collective-permute-start.27) | collective-permute-done | bytes 1048608 | tf_op jit(solution)/shard_map/ppermute | solution.py:23
  371.2 3.0 fusion.34
  374.3 1.5 bitcast_add_fusion.1
  376.0 1.6 collective-permute-start.42
  377.6 14.2 %collective-permute-done.21 = bf16[2,256,1024]{2,1,0:T(8,128)(2,1)S(1)} collective-permute-done((bf16[2,256,1024]{2,1,0:T(8,128)(2,1)}, bf16[2,256,1024]{2,1,0:T(8,128)(2,1)S(1)}, u32[]{:S(2)}, u32[]{:S(2)}) %collective-permute-start.21) | collective-permute-done | bytes 1048608 | tf_op jit(solution)/shard_map/ppermute | solution.py:23
  392.6 3.2 collective-permute-done.34
  395.8 4.3 collective-permute-start.22
  400.2 1.9 collective-permute-start.31
  404.2 5.9 %collective-permute-done.40 = bf16[128,1024]{1,0:T(8,128)(2,1)S(1)} collective-permute-done((bf16[128,1024]{1,0:T(8,128)(2,1)S(1)}, bf16[128,1024]{1,0:T(8,128)(2,1)S(1)}, u32[]{:S(2)}, u32[]{:S(2)}) %collective-permute-start.40) | collective-permute-done | bytes 262176 | tf_op jit(solution)/shard_map/ppermute | solution.py:27
  410.9 12.8 %collective-permute-done.22 = bf16[2,256,1024]{2,1,0:T(8,128)(2,1)S(1)} collective-permute-done((bf16[2,256,1024]{2,1,0:T(8,128)(2,1)S(1)}, bf16[2,256,1024]{2,1,0:T(8,128)(2,1)S(1)}, u32[]{:S(2)}, u32[]{:S(2)}) %collective-permute-start.22) | collective-permute-done | bytes 1048608 | tf_op jit(solution)/shard_map/ppermute | solution.py:23
  425.2 18.0 %collective-permute-done.31 = bf16[2,256,1024]{2,1,0:T(8,128)(2,1)S(1)} collective-permute-done((bf16[2,256,1024]{2,1,0:T(8,128)(2,1)S(1)}, bf16[2,256,1024]{2,1,0:T(8,128)(2,1)S(1)}, u32[]{:S(2)}, u32[]{:S(2)}) %collective-permute-start.31) | collective-permute-done | bytes 1048608 | tf_op jit(solution)/shard_map/ppermute | solution.py:23
  444.0 4.5 collective-permute-start.35
  453.7 5.5 %collective-permute-start.23 = (bf16[2,256,1024]{2,1,0:T(8,128)(2,1)S(1)}, bf16[2,256,1024]{2,1,0:T(8,128)(2,1)}, u32[]{:S(2)}, u32[]{:S(2)}) collective-permute-start(bf16[2,256,1024]{2,1,0:T(8,128)(2,1)S(1)} %get-tuple-element.64), channel_id=1, source_target_pairs={{0,1},{1,2},{2,3},{4,5},{5,6},{6,7},{8,9},{9,10},{10,11},{12,13},{... | collective-permute-start | bytes 3145736 | tf_op jit(solution)/shard_map/ppermute | solution.py:23
  462.0 10.0 %collective-permute-done.35 = bf16[2,256,1024]{2,1,0:T(8,128)(2,1)S(1)} collective-permute-done((bf16[2,256,1024]{2,1,0:T(8,128)(2,1)S(1)}, bf16[2,256,1024]{2,1,0:T(8,128)(2,1)S(1)}, u32[]{:S(2)}, u32[]{:S(2)}) %collective-permute-start.35) | collective-permute-done | bytes 1048608 | tf_op jit(solution)/shard_map/ppermute | solution.py:23
  472.0 4.6 collective-permute-done.36
  478.3 3.1 fusion.82
  482.0 8.6 %collective-permute-done.23 = bf16[2,256,1024]{2,1,0:T(8,128)(2,1)} collective-permute-done((bf16[2,256,1024]{2,1,0:T(8,128)(2,1)S(1)}, bf16[2,256,1024]{2,1,0:T(8,128)(2,1)}, u32[]{:S(2)}, u32[]{:S(2)}) %collective-permute-start.23) | collective-permute-done | bytes 1048608 | tf_op jit(solution)/shard_map/ppermute | solution.py:23
  490.6 4.5 collective-permute-done.26
  495.1 4.0 fusion.29
  (261 shorter events, 67.5 us)
Async XLA Ops:
  0.6 44.5 %collective-permute-start.1 = (bf16[2,256,1024]{2,1,0:T(8,128)(2,1)}, bf16[2,256,1024]{2,1,0:T(8,128)(2,1)}, u32[]{:S(2)}, u32[]{:S(2)}) collective-permute-start(bf16[2,256,1024]{2,1,0:T(8,128)(2,1)} %param.15), channel_id=1, source_target_pairs={{1,0},{2,1},{3,2},{5,4},{6,5},{7,6},{9,8},{10,9},{11,10},{13,12},{... | collective-permute-start | bytes 3145736 | tf_op jit(solution)/shard_map/ppermute | solution.py:23
  1.9 51.7 %collective-permute-start = (bf16[2,256,1024]{2,1,0:T(8,128)(2,1)}, bf16[2,256,1024]{2,1,0:T(8,128)(2,1)}, u32[]{:S(2)}, u32[]{:S(2)}) collective-permute-start(bf16[2,256,1024]{2,1,0:T(8,128)(2,1)} %param.15), channel_id=1, source_target_pairs={{0,1},{1,2},{2,3},{4,5},{5,6},{6,7},{8,9},{9,10},{10,11},{12,13},{... | collective-permute-start | bytes 3145736 | tf_op jit(solution)/shard_map/ppermute | solution.py:23
  8.5 17.6 %collective-permute-start.15 = (bf16[128,1024]{1,0:T(8,128)(2,1)}, bf16[128,1024]{1,0:T(8,128)(2,1)S(1)}, u32[]{:S(2)}, u32[]{:S(2)}) collective-permute-start(bf16[128,1024]{1,0:T(8,128)(2,1)} %param.25), channel_id=1, source_target_pairs={{0,16},{4,20},{8,24},{12,28},{16,0},{20,4},{24,8},{28,12},{1,17},{... | collective-permute-start | bytes 786440 | tf_op jit(solution)/shard_map/ppermute | solution.py:27
  10.5 17.4 %collective-permute-start.18 = (bf16[128,1024]{1,0:T(8,128)(2,1)}, bf16[128,1024]{1,0:T(8,128)(2,1)S(1)}, u32[]{:S(2)}, u32[]{:S(2)}) collective-permute-start(bf16[128,1024]{1,0:T(8,128)(2,1)} %param.27), channel_id=1, source_target_pairs={{0,8},{4,12},{8,0},{12,4},{16,24},{20,28},{24,16},{28,20},{1,9},{5... | collective-permute-start | bytes 786440 | tf_op jit(solution)/shard_map/ppermute | solution.py:27
  13.7 15.5 %collective-permute-start.6 = (bf16[128,1024]{1,0:T(8,128)(2,1)S(1)}, bf16[128,1024]{1,0:T(8,128)(2,1)}, u32[]{:S(2)}, u32[]{:S(2)}) collective-permute-start(bf16[128,1024]{1,0:T(8,128)(2,1)S(1)} %pad_maximum_fusion.9), channel_id=1, source_target_pairs={{0,8},{4,12},{8,0},{12,4},{16,24},{20,28},{24,16},{28,20},{1,9},{5... | collective-permute-start | bytes 786440 | tf_op jit(solution)/shard_map/ppermute | solution.py:27
  26.3 12.3 %collective-permute-start.16 = (bf16[2,128,1024]{2,1,0:T(8,128)(2,1)S(1)}, bf16[2,128,1024]{2,1,0:T(8,128)(2,1)S(1)}, u32[]{:S(2)}, u32[]{:S(2)}) collective-permute-start(bf16[2,128,1024]{2,1,0:T(8,128)(2,1)S(1)} %pad_maximum_fusion.6), channel_id=1, source_target_pairs={{0,8},{4,12},{8,0},{12,4},{16,24},{20,28},{24,16},{28,20},{1,9},{5... | collective-permute-start | bytes 1572872 | tf_op jit(solution)/shard_map/ppermute | solution.py:27
  28.7 15.2 %collective-permute-start.19 = (bf16[2,128,1024]{2,1,0:T(8,128)(2,1)}, bf16[2,128,1024]{2,1,0:T(8,128)(2,1)}, u32[]{:S(2)}, u32[]{:S(2)}) collective-permute-start(bf16[2,128,1024]{2,1,0:T(8,128)(2,1)} %pad_maximum_fusion.7), channel_id=1, source_target_pairs={{0,16},{4,20},{8,24},{12,28},{16,0},{20,4},{24,8},{28,12},{1,17},{... | collective-permute-start | bytes 1572872 | tf_op jit(solution)/shard_map/ppermute | solution.py:27
  31.2 21.1 %collective-permute-start.7 = (bf16[2,128,1024]{2,1,0:T(8,128)(2,1)}, bf16[2,128,1024]{2,1,0:T(8,128)(2,1)}, u32[]{:S(2)}, u32[]{:S(2)}) collective-permute-start(bf16[2,128,1024]{2,1,0:T(8,128)(2,1)} %pad_maximum_fusion.5), channel_id=1, source_target_pairs={{0,16},{4,20},{8,24},{12,28},{16,0},{20,4},{24,8},{28,12},{1,17},{... | collective-permute-start | bytes 1572872 | tf_op jit(solution)/shard_map/ppermute | solution.py:27
  39.8 15.3 %collective-permute-start.17 = (bf16[2,2,128,1024]{3,2,1,0:T(8,128)(2,1)}, bf16[2,2,128,1024]{3,2,1,0:T(8,128)(2,1)}, u32[]{:S(2)}, u32[]{:S(2)}) collective-permute-start(bf16[2,2,128,1024]{3,2,1,0:T(8,128)(2,1)} %pad_maximum_fusion.3), channel_id=1, source_target_pairs={{0,4},{4,0},{8,12},{12,8},{16,20},{20,16},{24,28},{28,24},{1,5},{5... | collective-permute-start | bytes 3145736 | tf_op jit(solution)/shard_map/ppermute | solution.py:27
  45.2 24.5 %collective-permute-start.2 = (bf16[2,256,1024]{2,1,0:T(8,128)(2,1)}, bf16[2,256,1024]{2,1,0:T(8,128)(2,1)}, u32[]{:S(2)}, u32[]{:S(2)}) collective-permute-start(bf16[2,256,1024]{2,1,0:T(8,128)(2,1)} %collective-permute-done.1), channel_id=1, source_target_pairs={{1,0},{2,1},{5,4},{6,5},{9,8},{10,9},{13,12},{14,13},{17,16},{18,1... | collective-permute-start | bytes 3145736 | tf_op jit(solution)/shard_map/ppermute | solution.py:23
  47.6 23.8 %collective-permute-start.20 = (bf16[2,2,128,1024]{3,2,1,0:T(8,128)(2,1)}, bf16[2,2,128,1024]{3,2,1,0:T(8,128)(2,1)}, u32[]{:S(2)}, u32[]{:S(2)}) collective-permute-start(bf16[2,2,128,1024]{3,2,1,0:T(8,128)(2,1)} %pad_maximum_fusion.4), channel_id=1, source_target_pairs={{0,4},{4,0},{8,12},{12,8},{16,20},{20,16},{24,28},{28,24},{1,5},{5... | collective-permute-start | bytes 3145736 | tf_op jit(solution)/shard_map/ppermute | solution.py:27
  53.6 21.2 %collective-permute-start.8 = (bf16[2,2,128,1024]{3,2,1,0:T(8,128)(2,1)S(1)}, bf16[2,2,128,1024]{3,2,1,0:T(8,128)(2,1)S(1)}, u32[]{:S(2)}, u32[]{:S(2)}) collective-permute-start(bf16[2,2,128,1024]{3,2,1,0:T(8,128)(2,1)S(1)} %pad_maximum_fusion.2), channel_id=1, source_target_pairs={{0,4},{4,0},{8,12},{12,8},{16,20},{20,16},{24,28},{28,24},{1,5},{5... | collective-permute-start | bytes 3145736 | tf_op jit(solution)/shard_map/ppermute | solution.py:27
  53.7 20.2 %collective-permute-start.4 = (bf16[2,256,1024]{2,1,0:T(8,128)(2,1)}, bf16[2,256,1024]{2,1,0:T(8,128)(2,1)S(1)}, u32[]{:S(2)}, u32[]{:S(2)}) collective-permute-start(bf16[2,256,1024]{2,1,0:T(8,128)(2,1)} %collective-permute-done), channel_id=1, source_target_pairs={{1,2},{2,3},{5,6},{6,7},{9,10},{10,11},{13,14},{14,15},{17,18},{18... | collective-permute-start | bytes 3145736 | tf_op jit(solution)/shard_map/ppermute | solution.py:23
  69.7 23.4 %collective-permute-start.3 = (bf16[2,256,1024]{2,1,0:T(8,128)(2,1)}, bf16[2,256,1024]{2,1,0:T(8,128)(2,1)S(1)}, u32[]{:S(2)}, u32[]{:S(2)}) collective-permute-start(bf16[2,256,1024]{2,1,0:T(8,128)(2,1)} %collective-permute-done.2), channel_id=1, source_target_pairs={{1,0},{5,4},{9,8},{13,12},{17,16},{21,20},{25,24},{29,28}} | collective-permute-start | bytes 3145736 | tf_op jit(solution)/shard_map/ppermute | solution.py:23
  71.3 33.5 %copy-start.20 = (bf16[2,2,2,128,1024]{4,3,2,1,0:T(8,128)(2,1)}, bf16[2,2,2,128,1024]{4,3,2,1,0:T(8,128)(2,1)S(1)}, u32[]{:S(2)}) copy-start(bf16[2,2,2,128,1024]{4,3,2,1,0:T(8,128)(2,1)S(1)} %copy.54) | copy-start | bytes 6291460
  73.9 86.9 %copy-start.22 = (bf16[2,2,2,128,1024]{4,3,2,1,0:T(8,128)(2,1)}, bf16[2,2,2,128,1024]{4,3,2,1,0:T(8,128)(2,1)S(1)}, u32[]{:S(2)}) copy-start(bf16[2,2,2,128,1024]{4,3,2,1,0:T(8,128)(2,1)S(1)} %copy.55) | copy-start | bytes 6291460
  73.9 19.2 %copy-start.1 = (bf16[2,4,256,1024]{3,2,1,0:T(8,128)(2,1)S(1)}, bf16[2,4,256,1024]{3,2,1,0:T(8,128)(2,1)}, u32[]{:S(2)}) copy-start(bf16[2,4,256,1024]{3,2,1,0:T(8,128)(2,1)} %copy-done) | copy-start | bytes 12582916
  73.9 21.3 %collective-permute-start.5 = (bf16[2,256,1024]{2,1,0:T(8,128)(2,1)S(1)}, bf16[2,256,1024]{2,1,0:T(8,128)(2,1)S(1)}, u32[]{:S(2)}, u32[]{:S(2)}) collective-permute-start(bf16[2,256,1024]{2,1,0:T(8,128)(2,1)S(1)} %collective-permute-done.4), channel_id=1, source_target_pairs={{2,3},{6,7},{10,11},{14,15},{18,19},{22,23},{26,27},{30,31}} | collective-permute-start | bytes 3145736 | tf_op jit(solution)/shard_map/ppermute | solution.py:23
  75.1 46.3 %copy-start.11 = (bf16[2,2,2,128,1024]{4,3,0,2,1:T(8,128)(2,1)}, bf16[2,2,2,128,1024]{4,3,0,2,1:T(8,128)(2,1)S(1)}, u32[]{:S(2)}) copy-start(bf16[2,2,2,128,1024]{4,3,0,2,1:T(8,128)(2,1)S(1)} %pad_maximum_fusion.1) | copy-start | bytes 6291460
  96.9 24.6 %copy-start.2 = (bf16[2,4,256,1024]{3,2,1,0:T(8,128)(2,1)}, bf16[2,4,256,1024]{3,2,1,0:T(8,128)(2,1)S(1)}, u32[]{:S(2)}) copy-start(bf16[2,4,256,1024]{3,2,1,0:T(8,128)(2,1)S(1)} %bitcast_dynamic-update-slice_fusion.4) | copy-start | bytes 12582916
  96.9 22.3 %collective-permute-start.10 = (bf16[2,256,1024]{2,1,0:T(8,128)(2,1)S(1)}, bf16[2,256,1024]{2,1,0:T(8,128)(2,1)S(1)}, u32[]{:S(2)}, u32[]{:S(2)}) collective-permute-start(bf16[2,256,1024]{2,1,0:T(8,128)(2,1)S(1)} %copy-done.7), channel_id=1, source_target_pairs={{1,0},{2,1},{3,2},{5,4},{6,5},{7,6},{9,8},{10,9},{11,10},{13,12},{... | collective-permute-start | bytes 3145736 | tf_op jit(solution)/shard_map/ppermute | solution.py:23
  98.2 22.3 %collective-permute-start.9 = (bf16[2,256,1024]{2,1,0:T(8,128)(2,1)S(1)}, bf16[2,256,1024]{2,1,0:T(8,128)(2,1)S(1)}, u32[]{:S(2)}, u32[]{:S(2)}) collective-permute-start(bf16[2,256,1024]{2,1,0:T(8,128)(2,1)S(1)} %copy-done.7), channel_id=1, source_target_pairs={{0,1},{1,2},{2,3},{4,5},{5,6},{6,7},{8,9},{9,10},{10,11},{12,13},{... | collective-permute-start | bytes 3145736 | tf_op jit(solution)/shard_map/ppermute | solution.py:23
  113.6 47.2 %copy-start.42 = (bf16[2048,1024]{1,0:T(8,128)(2,1)}, bf16[2048,1024]{1,0:T(8,128)(2,1)S(1)}, u32[]{:S(2)}) copy-start(bf16[2048,1024]{1,0:T(8,128)(2,1)S(1)} %get-tuple-element.104) | copy-start | bytes 12582916
  119.2 39.5 %collective-permute-start.11 = (bf16[2,256,1024]{2,1,0:T(8,128)(2,1)S(1)}, bf16[2,256,1024]{2,1,0:T(8,128)(2,1)S(1)}, u32[]{:S(2)}, u32[]{:S(2)}) collective-permute-start(bf16[2,256,1024]{2,1,0:T(8,128)(2,1)S(1)} %collective-permute-done.10), channel_id=1, source_target_pairs={{1,0},{2,1},{5,4},{6,5},{9,8},{10,9},{13,12},{14,13},{17,16},{18,1... | collective-permute-start | bytes 3145736 | tf_op jit(solution)/shard_map/ppermute | solution.py:23
  120.5 39.5 %collective-permute-start.13 = (bf16[2,256,1024]{2,1,0:T(8,128)(2,1)S(1)}, bf16[2,256,1024]{2,1,0:T(8,128)(2,1)S(1)}, u32[]{:S(2)}, u32[]{:S(2)}) collective-permute-start(bf16[2,256,1024]{2,1,0:T(8,128)(2,1)S(1)} %collective-permute-done.9), channel_id=1, source_target_pairs={{1,2},{2,3},{5,6},{6,7},{9,10},{10,11},{13,14},{14,15},{17,18},{18... | collective-permute-start | bytes 3145736 | tf_op jit(solution)/shard_map/ppermute | solution.py:23
  158.7 24.7 %collective-permute-start.12 = (bf16[2,256,1024]{2,1,0:T(8,128)(2,1)S(1)}, bf16[2,256,1024]{2,1,0:T(8,128)(2,1)S(1)}, u32[]{:S(2)}, u32[]{:S(2)}) collective-permute-start(bf16[2,256,1024]{2,1,0:T(8,128)(2,1)S(1)} %collective-permute-done.11), channel_id=1, source_target_pairs={{1,0},{5,4},{9,8},{13,12},{17,16},{21,20},{25,24},{29,28}} | collective-permute-start | bytes 3145736 | tf_op jit(solution)/shard_map/ppermute | solution.py:23
  160.0 26.2 %collective-permute-start.14 = (bf16[2,256,1024]{2,1,0:T(8,128)(2,1)S(1)}, bf16[2,256,1024]{2,1,0:T(8,128)(2,1)S(1)}, u32[]{:S(2)}, u32[]{:S(2)}) collective-permute-start(bf16[2,256,1024]{2,1,0:T(8,128)(2,1)S(1)} %collective-permute-done.13), channel_id=1, source_target_pairs={{2,3},{6,7},{10,11},{14,15},{18,19},{22,23},{26,27},{30,31}} | collective-permute-start | bytes 3145736 | tf_op jit(solution)/shard_map/ppermute | solution.py:23
  227.5 123.1 %collective-permute-start.44 = (bf16[2,2,128,1024]{3,2,1,0:T(8,128)(2,1)}, bf16[2,2,128,1024]{3,2,1,0:T(8,128)(2,1)}, u32[]{:S(2)}, u32[]{:S(2)}) collective-permute-start(bf16[2,2,128,1024]{3,2,1,0:T(8,128)(2,1)} %fusion.50), channel_id=1, source_target_pairs={{0,4},{4,0},{8,12},{12,8},{16,20},{20,16},{24,28},{28,24},{1,5},{5... | collective-permute-start | bytes 3145736 | tf_op jit(solution)/shard_map/ppermute | solution.py:27
  228.8 145.4 %collective-permute-start.41 = (bf16[2,2,128,1024]{3,2,1,0:T(8,128)(2,1)}, bf16[2,2,128,1024]{3,2,1,0:T(8,128)(2,1)}, u32[]{:S(2)}, u32[]{:S(2)}) collective-permute-start(bf16[2,2,128,1024]{3,2,1,0:T(8,128)(2,1)} %fusion.55), channel_id=1, source_target_pairs={{0,4},{4,0},{8,12},{12,8},{16,20},{20,16},{24,28},{28,24},{1,5},{5... | collective-permute-start | bytes 3145736 | tf_op jit(solution)/shard_map/ppermute | solution.py:27
  303.2 44.0 %collective-permute-start.38 = (bf16[2,2,128,1024]{3,2,1,0:T(8,128)(2,1)}, bf16[2,2,128,1024]{3,2,1,0:T(8,128)(2,1)S(1)}, u32[]{:S(2)}, u32[]{:S(2)}) collective-permute-start(bf16[2,2,128,1024]{3,2,1,0:T(8,128)(2,1)} %bitcast.285), channel_id=1, source_target_pairs={{0,4},{4,0},{8,12},{12,8},{16,20},{20,16},{24,28},{28,24},{1,5},{5... | collective-permute-start | bytes 3145736 | tf_op jit(solution)/shard_map/ppermute | solution.py:27
  322.8 9.0 %collective-permute-start.29 = (f32[96,128]{1,0:T(8,128)S(1)}, f32[96,128]{1,0:T(8,128)S(1)}, u32[]{:S(2)}, u32[]{:S(2)}) collective-permute-start(f32[96,128]{1,0:T(8,128)S(1)} %bitcast.286), channel_id=1, source_target_pairs={{0,1},{1,0},{2,3},{3,2},{4,5},{5,4},{6,7},{7,6},{8,9},{9,8},{10,11... | collective-permute-start | bytes 147464 | tf_op jit(solution)/shard_map/ppermute | solution.py:27
  331.8 14.6 %collective-permute-start.30 = (f32[96,128]{1,0:T(8,128)S(1)}, f32[96,128]{1,0:T(8,128)S(1)}, u32[]{:S(2)}, u32[]{:S(2)}) collective-permute-start(f32[96,128]{1,0:T(8,128)S(1)} %bitcast_add_fusion.19), channel_id=1, source_target_pairs={{0,2},{1,3},{2,0},{3,1},{4,6},{5,7},{6,4},{7,5},{8,10},{9,11},{10,... | collective-permute-start | bytes 147464 | tf_op jit(solution)/shard_map/ppermute | solution.py:27
  344.1 26.0 %collective-permute-start.27 = (bf16[2,256,1024]{2,1,0:T(8,128)(2,1)}, bf16[2,256,1024]{2,1,0:T(8,128)(2,1)S(1)}, u32[]{:S(2)}, u32[]{:S(2)}) collective-permute-start(bf16[2,256,1024]{2,1,0:T(8,128)(2,1)} %get-tuple-element.63), channel_id=1, source_target_pairs={{0,1},{4,5},{8,9},{12,13},{16,17},{20,21},{24,25},{28,29}} | collective-permute-start | bytes 3145736 | tf_op jit(solution)/shard_map/ppermute | solution.py:23
  346.4 24.3 %collective-permute-start.28 = (bf16[2,256,1024]{2,1,0:T(8,128)(2,1)}, bf16[2,256,1024]{2,1,0:T(8,128)(2,1)S(1)}, u32[]{:S(2)}, u32[]{:S(2)}) collective-permute-start(bf16[2,256,1024]{2,1,0:T(8,128)(2,1)} %get-tuple-element.62), channel_id=1, source_target_pairs={{3,2},{7,6},{11,10},{15,14},{19,18},{23,22},{27,26},{31,30}} | collective-permute-start | bytes 3145736 | tf_op jit(solution)/shard_map/ppermute | solution.py:23
  347.2 44.6 %collective-permute-start.21 = (bf16[2,256,1024]{2,1,0:T(8,128)(2,1)}, bf16[2,256,1024]{2,1,0:T(8,128)(2,1)S(1)}, u32[]{:S(2)}, u32[]{:S(2)}) collective-permute-start(bf16[2,256,1024]{2,1,0:T(8,128)(2,1)} %get-tuple-element.66), channel_id=1, source_target_pairs={{0,1},{4,5},{8,9},{12,13},{16,17},{20,21},{24,25},{28,29}} | collective-permute-start | bytes 3145736 | tf_op jit(solution)/shard_map/ppermute | solution.py:23
  350.6 59.7 %collective-permute-start.24 = (bf16[2,256,1024]{2,1,0:T(8,128)(2,1)S(1)}, bf16[2,256,1024]{2,1,0:T(8,128)(2,1)S(1)}, u32[]{:S(2)}, u32[]{:S(2)}) collective-permute-start(bf16[2,256,1024]{2,1,0:T(8,128)(2,1)S(1)} %get-tuple-element.67), channel_id=1, source_target_pairs={{3,2},{7,6},{11,10},{15,14},{19,18},{23,22},{27,26},{31,30}} | collective-permute-start | bytes 3145736 | tf_op jit(solution)/shard_map/ppermute | solution.py:23
  352.9 39.4 %slice-start = ((s8[8388608]{0:T(1024)(128)(4,1)}), s8[4194304]{0:T(1024)(128)(4,1)S(1)}, s32[]{:S(2)}) async-start(s8[8388608]{0:T(1024)(128)(4,1)} %bitcast.254), calls=%async_computation | async-start | bytes 8388608
  353.0 21.3 %copy-start.14 = (f32[1024,1024]{1,0:T(8,128)S(1)}, f32[1024,1024]{1,0:T(8,128)}, u32[]{:S(2)}) copy-start(f32[1024,1024]{1,0:T(8,128)} %copy-done.13) | copy-start | bytes 12582916
  353.1 39.2 %slice-start.1 = ((s8[8388608]{0:T(1024)(128)(4,1)}), s8[4194304]{0:T(1024)(128)(4,1)S(1)}, s32[]{:S(2)}) async-start(s8[8388608]{0:T(1024)(128)(4,1)} %bitcast.254), calls=%async_computation.1 | async-start | bytes 8388608
  370.2 33.1 %collective-permute-start.45 = (bf16[2,128,1024]{2,1,0:T(8,128)(2,1)S(1)}, bf16[2,128,1024]{2,1,0:T(8,128)(2,1)S(1)}, u32[]{:S(2)}, u32[]{:S(2)}) collective-permute-start(bf16[2,128,1024]{2,1,0:T(8,128)(2,1)S(1)} %fusion.58), channel_id=1, source_target_pairs={{0,8},{4,12},{8,0},{12,4},{16,24},{20,28},{24,16},{28,20},{1,9},{5... | collective-permute-start | bytes 1572872 | tf_op jit(solution)/shard_map/ppermute | solution.py:27
  370.7 29.5 %collective-permute-start.39 = (bf16[2,128,1024]{2,1,0:T(8,128)(2,1)S(1)}, bf16[2,128,1024]{2,1,0:T(8,128)(2,1)S(1)}, u32[]{:S(2)}, u32[]{:S(2)}) collective-permute-start(bf16[2,128,1024]{2,1,0:T(8,128)(2,1)S(1)} %fusion.56), channel_id=1, source_target_pairs={{0,16},{4,20},{8,24},{12,28},{16,0},{20,4},{24,8},{28,12},{1,17},{... | collective-permute-start | bytes 1572872 | tf_op jit(solution)/shard_map/ppermute | solution.py:27
  374.2 1.7 collective-permute-start.33
  376.0 26.4 %collective-permute-start.42 = (bf16[2,128,1024]{2,1,0:T(8,128)(2,1)S(1)}, bf16[2,128,1024]{2,1,0:T(8,128)(2,1)S(1)}, u32[]{:S(2)}, u32[]{:S(2)}) collective-permute-start(bf16[2,128,1024]{2,1,0:T(8,128)(2,1)S(1)} %fusion.57), channel_id=1, source_target_pairs={{0,16},{4,20},{8,24},{12,28},{16,0},{20,4},{24,8},{28,12},{1,17},{... | collective-permute-start | bytes 1572872 | tf_op jit(solution)/shard_map/ppermute | solution.py:27
  391.7 4.1 collective-permute-start.34
  395.8 27.9 %collective-permute-start.22 = (bf16[2,256,1024]{2,1,0:T(8,128)(2,1)S(1)}, bf16[2,256,1024]{2,1,0:T(8,128)(2,1)S(1)}, u32[]{:S(2)}, u32[]{:S(2)}) collective-permute-start(bf16[2,256,1024]{2,1,0:T(8,128)(2,1)S(1)} %fusion.40), channel_id=1, source_target_pairs={{0,1},{1,2},{4,5},{5,6},{8,9},{9,10},{12,13},{13,14},{16,17},{17,1... | collective-permute-start | bytes 3145736 | tf_op jit(solution)/shard_map/ppermute | solution.py:23
  400.2 43.0 %collective-permute-start.31 = (bf16[2,256,1024]{2,1,0:T(8,128)(2,1)S(1)}, bf16[2,256,1024]{2,1,0:T(8,128)(2,1)S(1)}, u32[]{:S(2)}, u32[]{:S(2)}) collective-permute-start(bf16[2,256,1024]{2,1,0:T(8,128)(2,1)S(1)} %get-tuple-element.58), channel_id=1, source_target_pairs={{0,1},{1,2},{4,5},{5,6},{8,9},{9,10},{12,13},{13,14},{16,17},{17,1... | collective-permute-start | bytes 3145736 | tf_op jit(solution)/shard_map/ppermute | solution.py:23
  402.4 40.9 %collective-permute-start.32 = (bf16[2,256,1024]{2,1,0:T(8,128)(2,1)S(1)}, bf16[2,256,1024]{2,1,0:T(8,128)(2,1)S(1)}, u32[]{:S(2)}, u32[]{:S(2)}) collective-permute-start(bf16[2,256,1024]{2,1,0:T(8,128)(2,1)S(1)} %get-tuple-element.57), channel_id=1, source_target_pairs={{3,2},{2,1},{7,6},{6,5},{11,10},{10,9},{15,14},{14,13},{19,18},{18... | collective-permute-start | bytes 3145736 | tf_op jit(solution)/shard_map/ppermute | solution.py:23
  403.1 40.1 %slice-start.2 = ((s8[8388608]{0:T(1024)(128)(4,1)}), s8[4194304]{0:T(1024)(128)(4,1)S(1)}, s32[]{:S(2)}) async-start(s8[8388608]{0:T(1024)(128)(4,1)} %bitcast.269), calls=%async_computation.2 | async-start | bytes 8388608
  403.3 6.7 %collective-permute-start.40 = (bf16[128,1024]{1,0:T(8,128)(2,1)S(1)}, bf16[128,1024]{1,0:T(8,128)(2,1)S(1)}, u32[]{:S(2)}, u32[]{:S(2)}) collective-permute-start(bf16[128,1024]{1,0:T(8,128)(2,1)S(1)} %fusion.61), channel_id=1, source_target_pairs={{0,8},{4,12},{8,0},{12,4},{16,24},{20,28},{24,16},{28,20},{1,9},{5... | collective-permute-start | bytes 786440 | tf_op jit(solution)/shard_map/ppermute | solution.py:27
  410.0 40.6 %collective-permute-start.46 = (bf16[128,1024]{1,0:T(8,128)(2,1)S(1)}, bf16[128,1024]{1,0:T(8,128)(2,1)S(1)}, u32[]{:S(2)}, u32[]{:S(2)}) collective-permute-start(bf16[128,1024]{1,0:T(8,128)(2,1)S(1)} %fusion.63), channel_id=1, source_target_pairs={{0,16},{4,20},{8,24},{12,28},{16,0},{20,4},{24,8},{28,12},{1,17},{... | collective-permute-start | bytes 786440 | tf_op jit(solution)/shard_map/ppermute | solution.py:27
  410.3 32.9 %slice-start.3 = ((s8[8388608]{0:T(1024)(128)(4,1)}), s8[4194304]{0:T(1024)(128)(4,1)S(1)}, s32[]{:S(2)}) async-start(s8[8388608]{0:T(1024)(128)(4,1)} %bitcast.269), calls=%async_computation.3 | async-start | bytes 8388608
  410.3 41.2 %collective-permute-start.43 = (bf16[128,1024]{1,0:T(8,128)(2,1)S(1)}, bf16[128,1024]{1,0:T(8,128)(2,1)S(1)}, u32[]{:S(2)}, u32[]{:S(2)}) collective-permute-start(bf16[128,1024]{1,0:T(8,128)(2,1)S(1)} %fusion.62), channel_id=1, source_target_pairs={{0,8},{4,12},{8,0},{12,4},{16,24},{20,28},{24,16},{28,20},{1,9},{5... | collective-permute-start | bytes 786440 | tf_op jit(solution)/shard_map/ppermute | solution.py:27
  424.4 34.8 %collective-permute-start.25 = (bf16[2,256,1024]{2,1,0:T(8,128)(2,1)S(1)}, bf16[2,256,1024]{2,1,0:T(8,128)(2,1)S(1)}, u32[]{:S(2)}, u32[]{:S(2)}) collective-permute-start(bf16[2,256,1024]{2,1,0:T(8,128)(2,1)S(1)} %get-tuple-element.65), channel_id=1, source_target_pairs={{3,2},{2,1},{7,6},{6,5},{11,10},{10,9},{15,14},{14,13},{19,18},{18... | collective-permute-start | bytes 3145736 | tf_op jit(solution)/shard_map/ppermute | solution.py:23
  444.0 28.0 %collective-permute-start.35 = (bf16[2,256,1024]{2,1,0:T(8,128)(2,1)S(1)}, bf16[2,256,1024]{2,1,0:T(8,128)(2,1)S(1)}, u32[]{:S(2)}, u32[]{:S(2)}) collective-permute-start(bf16[2,256,1024]{2,1,0:T(8,128)(2,1)S(1)} %get-tuple-element.56), channel_id=1, source_target_pairs={{0,1},{1,2},{2,3},{4,5},{5,6},{6,7},{8,9},{9,10},{10,11},{12,13},{... | collective-permute-start | bytes 3145736 | tf_op jit(solution)/shard_map/ppermute | solution.py:23
  448.5 29.8 %copy-start.6 = (bf16[2,256,1024]{2,1,0:T(8,128)(2,1)S(1)}, bf16[2,256,1024]{2,1,0:T(8,128)(2,1)}, u32[]{:S(2)}) copy-start(bf16[2,256,1024]{2,1,0:T(8,128)(2,1)} %param.15) | copy-start | bytes 3145732
  448.5 29.8 %copy-start.30 = (f32[2,256]{1,0:T(2,128)S(1)}, f32[2,256]{1,0:T(2,128)}, u32[]{:S(2)}) copy-start(f32[2,256]{1,0:T(2,128)} %copy-done.29) | copy-start | bytes 6148
  448.5 29.8 %copy-start.31 = (f32[2,256]{1,0:T(2,128)S(1)}, f32[2,256]{1,0:T(2,128)}, u32[]{:S(2)}) copy-start(f32[2,256]{1,0:T(2,128)} %add_rsqrt_fusion.1) | copy-start | bytes 6148
  448.5 28.1 %collective-permute-start.36 = (bf16[2,256,1024]{2,1,0:T(8,128)(2,1)S(1)}, bf16[2,256,1024]{2,1,0:T(8,128)(2,1)S(1)}, u32[]{:S(2)}, u32[]{:S(2)}) collective-permute-start(bf16[2,256,1024]{2,1,0:T(8,128)(2,1)S(1)} %get-tuple-element.55), channel_id=1, source_target_pairs={{3,2},{2,1},{1,0},{7,6},{6,5},{5,4},{11,10},{10,9},{9,8},{15,14},{... | collective-permute-start | bytes 3145736 | tf_op jit(solution)/shard_map/ppermute | solution.py:23
  452.4 6.8 %collective-permute-start.37 = (f32[96,128]{1,0:T(8,128)S(1)}, f32[96,128]{1,0:T(8,128)S(1)}, u32[]{:S(2)}, u32[]{:S(2)}) collective-permute-start(f32[96,128]{1,0:T(8,128)S(1)} %add.374), channel_id=1, source_target_pairs={{0,16},{4,20},{8,24},{12,28},{16,0},{20,4},{24,8},{28,12},{1,17},{... | collective-permute-start | bytes 147464 | tf_op jit(solution)/shard_map/ppermute | solution.py:27
  453.7 36.9 %collective-permute-start.23 = (bf16[2,256,1024]{2,1,0:T(8,128)(2,1)S(1)}, bf16[2,256,1024]{2,1,0:T(8,128)(2,1)}, u32[]{:S(2)}, u32[]{:S(2)}) collective-permute-start(bf16[2,256,1024]{2,1,0:T(8,128)(2,1)S(1)} %get-tuple-element.64), channel_id=1, source_target_pairs={{0,1},{1,2},{2,3},{4,5},{5,6},{6,7},{8,9},{9,10},{10,11},{12,13},{... | collective-permute-start | bytes 3145736 | tf_op jit(solution)/shard_map/ppermute | solution.py:23
  460.6 34.5 %copy-start.32 = (f32[1024]{0:T(1024)S(1)}, f32[1024]{0:T(1024)}, u32[]{:S(2)}) copy-start(f32[1024]{0:T(1024)} %convert_element_type.283) | copy-start | bytes 12292
  460.6 34.5 %copy-start.33 = (f32[1024]{0:T(1024)S(1)}, f32[1024]{0:T(1024)}, u32[]{:S(2)}) copy-start(f32[1024]{0:T(1024)} %convert_element_type.284) | copy-start | bytes 12292
  460.6 34.5 %collective-permute-start.26 = (bf16[2,256,1024]{2,1,0:T(8,128)(2,1)}, bf16[2,256,1024]{2,1,0:T(8,128)(2,1)}, u32[]{:S(2)}, u32[]{:S(2)}) collective-permute-start(bf16[2,256,1024]{2,1,0:T(8,128)(2,1)} %fusion.39), channel_id=1, source_target_pairs={{3,2},{2,1},{1,0},{7,6},{6,5},{5,4},{11,10},{10,9},{9,8},{15,14},{... | collective-permute-start | bytes 3145736 | tf_op jit(solution)/shard_map/ppermute | solution.py:23
  477.6 21.4 %copy-start.35 = (f32[1024]{0:T(1024)}, f32[1024]{0:T(1024)S(1)}, u32[]{:S(2)}) copy-start(f32[1024]{0:T(1024)S(1)} %get-tuple-element.135) | copy-start | bytes 12292
  (31 other events, 235.4 us)
